TPU v7x, 256 devices: a whole 4x4x8 slice. The times are simulated.
256 devices in a mesh: replica: 8 (over y, core), tensor: 32 (over x, z).
Axes of the slice: x: 4, y: 4, z: 8, core: 2. Of those that a mesh axis runs over, the one named last changes fastest.
Arguments:
- tokens: bfloat16 [1024, 2560], P('replica', 'tensor'), may hold values from -6 to 6
- next_tokens: bfloat16 [512, 2560], P('replica', 'tensor'), may hold values from -6 to 6
- cotangent: bfloat16 [1024, 2560], P('replica', 'tensor'), may hold values from -0.5 to 0.5
- gate_weight: bfloat16 [2560, 14336], P(None, 'tensor'), may hold values from -0.125 to 0.125
- up_weight: bfloat16 [2560, 14336], P(None, 'tensor'), may hold values from -0.125 to 0.125
- down_weight: bfloat16 [14336, 2560], P('tensor'), may hold values from -0.046875 to 0.046875
- momentum: bfloat16 [8, 14336, 2560], P('replica', 'tensor'), may hold values from -6 to 6
- indices: int32 [8, 224, 40, 32], P(None, 'tensor'), may hold values from 0 to 4095, as said below
Outputs:
- output: bfloat16 [512, 2560], P(('replica', 'tensor'))
- new_momentum: bfloat16 [8, 14336, 2560], P('replica', 'tensor')
Inputs may be any that keep to these rules, and one draw needn't show every extreme that they name: Within one replica and tile the 32 indices are distinct; the n-th lies in the range from n * 64 * 2 to (n + 1) * 64 * 2 - 1.
All inputs are finite; a program needn't handle non-finite values.
Results may differ from a plain program's by a relative error of at most 0.017.
Values may be sent and summed in bfloat16 or wider, within the bound.
No kernel may reach another device: no remote copies, remote signals or barrier semaphores. Data moves between devices by JAX's collectives and lax.ppermute only.
A program may use at most 128 MiB of HBM per device.

v0:
```python
import jax
import jax.numpy as jnp
from jax import lax
from jax.sharding import PartitionSpec as P

TILE = 64


BETA_DECAY = 0.9
STEP_RATE = 0.1


def cosine_table():
    freq = jnp.arange(TILE, dtype=jnp.float32)[:, None]
    place = jnp.arange(TILE, dtype=jnp.float32)[None, :]
    table = jnp.cos(jnp.pi * (2.0 * place + 1.0) * freq / (2.0 * TILE))
    factor = jnp.where(freq == 0.0, jnp.sqrt(1.0 / TILE), jnp.sqrt(2.0 / TILE))
    return table * factor


def forward_tiles(field, table):
    height, breadth = field.shape
    blocks = field.reshape(height // TILE, TILE, breadth // TILE, TILE)
    spectrum = jnp.einsum("ak,xkyl,bl->xyab", table, blocks, table, precision=lax.Precision.HIGHEST)
    return spectrum.reshape(height // TILE, breadth // TILE, TILE * TILE)


def inverse_tiles(spectrum, table):
    tile_rows, tile_cols, _ = spectrum.shape
    blocks = spectrum.reshape(tile_rows, tile_cols, TILE, TILE)
    field = jnp.einsum("ak,xyab,bl->xkyl", table, blocks, table, precision=lax.Precision.HIGHEST)
    return field.reshape(tile_rows * TILE, tile_cols * TILE)


def one_hot_slots(where):
    keep_count = where.shape[-1]
    stride = TILE * TILE // keep_count
    offset = where - jnp.arange(keep_count, dtype=jnp.int32) * stride
    slots = jnp.arange(stride, dtype=jnp.int32)
    return (offset[..., None] == slots).astype(jnp.float32)


def pick_values(spectrum, where):
    tile_rows, tile_cols, keep_count = where.shape
    grid = spectrum.reshape(tile_rows, tile_cols, keep_count, TILE * TILE // keep_count)
    return jnp.sum(grid * one_hot_slots(where), axis=3)


def place_values(values, where):
    tile_rows, tile_cols, _ = where.shape
    placed = values[..., None] * one_hot_slots(where)
    return placed.reshape(tile_rows, tile_cols, TILE * TILE)


def place_listed(listed, where):
    replicas = where.shape[0]
    tile_rows, tile_cols = (where.shape[1], where.shape[2])

    def add_replica(step, dense):
        values = lax.dynamic_index_in_dim(listed, step, 0, keepdims=False).astype(jnp.float32)
        spots = lax.dynamic_index_in_dim(where, step, 0, keepdims=False)
        return dense + place_values(values, spots)

    dense = jnp.zeros((tile_rows, tile_cols, TILE * TILE), jnp.float32)
    return lax.fori_loop(0, replicas, add_replica, dense)


def swiglu(inputs, gate_weight, up_weight):
    gate = jnp.dot(inputs, gate_weight, preferred_element_type=jnp.float32)
    upper = jnp.dot(inputs, up_weight, preferred_element_type=jnp.float32)
    return (jax.nn.silu(gate) * upper).astype(jnp.bfloat16)


def on_device(
    tokens, next_tokens, cotangent, gate_weight, up_weight, down_weight, momentum, indices
):
    table = cosine_table()
    whole, whole_next, whole_grads = (
        lax.all_gather(tokens, "tensor", axis=1, tiled=True),
        lax.all_gather(next_tokens, "tensor", axis=1, tiled=True),
        lax.all_gather(cotangent, "tensor", axis=1, tiled=True),
    )
    hidden = swiglu(whole, gate_weight, up_weight)
    grad = lax.dot_general(
        hidden, whole_grads, (((0,), (0,)), ((), ())), preferred_element_type=jnp.float32
    )
    moment = BETA_DECAY * momentum[0].astype(jnp.float32) + grad
    spectrum = forward_tiles(moment, table)
    replica = lax.axis_index("replica")
    replicas = lax.axis_size("replica")
    own_where = lax.dynamic_index_in_dim(indices, replica, 0, keepdims=False)
    sent = pick_values(spectrum, own_where).astype(jnp.bfloat16)
    own = place_values(sent.astype(jnp.float32), own_where)
    kept = (moment - inverse_tiles(own, table)).astype(jnp.bfloat16)
    next_hidden = swiglu(whole_next, gate_weight, up_weight)
    listed = lax.all_gather(sent[None], "replica", axis=0, tiled=True)
    total = place_listed(listed, indices)
    update = inverse_tiles(total, table) / replicas
    new_down = (down_weight.astype(jnp.float32) - STEP_RATE * update).astype(jnp.bfloat16)
    output = lax.psum_scatter(
        jnp.dot(next_hidden, new_down, preferred_element_type=jnp.float32).astype(jnp.bfloat16),
        "tensor",
        scatter_dimension=0,
        tiled=True,
    )
    return (output, kept[None])


def solution(mesh):
    return jax.shard_map(
        on_device,
        mesh=mesh,
        in_specs=(
            P("replica", "tensor"),
            P("replica", "tensor"),
            P("replica", "tensor"),
            P(None, "tensor"),
            P(None, "tensor"),
            P("tensor", None),
            P("replica", "tensor", None),
            P(None, "tensor", None, None),
        ),
        out_specs=(P(("replica", "tensor"), None), P("replica", "tensor", None)),
        check_vma=False,
    )
```

profile of v0, /device:TPU:32, one launch (start us, length us, event | category | flops | bytes accessed | tf_op | source)
XLA Modules:
  0.0 656.7 jit_solution(2260627077995073052)
XLA Ops:
  7.3 52.0 %all_gather.13 = bf16[128,2560]{0,1:T(8,128)(2,1)S(1)} all-gather(bf16[128,80]{0,1:T(8,128)(2,1)} %param.10), channel_id=1, replica_groups=mesh['replica'=8,'tensor'=32] {'tensor'}, dimensions={1}, use_global_device_ids=true | all-gather | bytes 675840 | tf_op jit(solution)/shard_map/all_gather | solution.py:79
  59.3 52.1 %all_gather.14 = bf16[128,2560]{0,1:T(8,128)(2,1)} all-gather(bf16[128,80]{0,1:T(8,128)(2,1)} %param.12), channel_id=1, replica_groups=mesh['replica'=8,'tensor'=32] {'tensor'}, dimensions={1}, use_global_device_ids=true | all-gather | bytes 675840 | tf_op jit(solution)/shard_map/all_gather | solution.py:81
  113.9 6.6 %convolution_add_fusion = f32[448,2560]{1,0:T(8,128)} fusion(bf16[128,2560]{0,1:T(8,128)(2,1)} %all_gather.14, bf16[1,448,2560]{2,1,0:T(8,128)(2,1)} %param.16, bf16[2560,448]{0,1:T(8,128)(2,1)S(1)} %copy-done, bf16[128,2560]{0,1:T(8,128)(2,1)S(1)} %all_gather.13, f32[128,448]{0,1:T(8,128)S(1)} %fusion.58), kind=kOutput, calls=%fused_computation.14 | convolution fusion | flops 590987264 | bytes 10715136 | tf_op jit(solution)/shard_map/dot_general | solution.py:84
  120.4 7.7 %reshape.98 = f32[7,64,40,64]{3,2,1,0:T(8,128)} reshape(f32[448,2560]{1,0:T(8,128)} %convolution_add_fusion) | data formatting | bytes 9175040 | tf_op jit(solution)/shard_map/reshape | solution.py:23
  129.4 18.2 %fusion.2 = f32[7,40,64,64]{3,2,1,0:T(8,128)S(1)} fusion(f32[7,64,40,64]{3,2,1,0:T(8,128)} %reshape.98, f32[64]{0:T(128)S(1)} %get-tuple-element.117, f32[64]{0:T(128)S(1)} %get-tuple-element.118), kind=kOutput, calls=%fused_computation.11 | convolution fusion | flops 880816128 | bytes 9175552 | tf_op jit(solution)/shard_map/ak,xkyl,bl->xyab/dot_general | solution.py:24
  147.6 10.0 %fusion = f32[7,40,64]{2,1,0:T(8,128)S(1)} fusion(s32[64,64]{0,1:T(8,128)S(1)} %copy.22, s32[7,40,64]{2,1,0:T(8,128)S(1)} %copy.21, f32[7,40,64,64]{3,2,1,0:T(8,128)S(1)} %fusion.2, f32[64]{0:T(128)S(1)} %get-tuple-element.117, f32[64]{0:T(128)S(1)} %get-tuple-element.118), kind=kOutput, calls=%fused_computation.9 | convolution fusion | flops 884238848 | bytes 4747776 | tf_op jit(solution)/shard_map/ak,xkyl,bl->xyab/dot_general | solution.py:24
  158.1 13.6 %all-gather = bf16[56,40,32]{1,2,0:T(8,128)(2,1)S(1)} all-gather(bf16[7,40,32]{1,2,0:T(8,128)(2,1)S(1)} %reduce_sum.18), channel_id=2, replica_groups=mesh['replica'=8,'tensor'=32] {'replica'}, dimensions={0}, use_global_device_ids=true | all-gather | bytes 161280 | tf_op jit(solution)/shard_map/all_gather | solution.py:96
  171.6 228.8 %while.14 = (s32[]{:T(128)}, f32[7,40,4096]{2,1,0:T(8,128)}, s32[8,7,40,32]{2,3,1,0:T(8,128)}, bf16[8,7,40,32]{2,3,1,0:T(8,128)(2,1)S(1)}, s32[]{:T(128)}, /*index=5*/s32[]{:T(128)}) while((s32[]{:T(128)}, f32[7,40,4096]{2,1,0:T(8,128)}, s32[8,7,40,32]{2,3,1,0:T(8,128)}, bf16[8,7,40,32]{2,3,1,0:T(8,128)(2,1)S(1)}, s32[]{:T(128)}, ...), condition=%wide.region_3.4_spmd.clone, body=%wide.region_2.3_spmd.clone.sunk | while | flops 4605475 | bytes 46320468 | solution.py:65
  173.1 4.4 eq.144
  177.4 5.8 eq.145
  186.2 5.8 mul.382
  192.0 7.4 %select_add_fusion.2 = f32[7,40,4096]{2,1,0:T(8,128)} fusion(f32[7,40,4096]{2,1,0:T(8,128)} %get-tuple-element.151, f32[7,40,4096]{2,1,0:T(8,128)} %mul.382, s32[7,40,4096]{2,1,0:T(8,128)} %eq.145, s32[4096]{0:T(1024)S(1)} %iota_bitcast_fusion.2, pred[]{:T(512)S(6)} %compare.3), kind=kLoop, calls=%fused_computation.clone.1 | loop fusion | flops 4587520 | bytes 18366464 | tf_op jit(solution)/shard_map/while/body/eval_jaxpr/add | solution.py:62
  204.8 5.8 eq.145
  213.6 5.8 mul.382
  219.4 8.7 %select_add_fusion.2 = f32[7,40,4096]{2,1,0:T(8,128)} fusion(f32[7,40,4096]{2,1,0:T(8,128)} %get-tuple-element.151, f32[7,40,4096]{2,1,0:T(8,128)} %mul.382, s32[7,40,4096]{2,1,0:T(8,128)} %eq.145, s32[4096]{0:T(1024)S(1)} %iota_bitcast_fusion.2, pred[]{:T(512)S(6)} %compare.3), kind=kLoop, calls=%fused_computation.clone.1 | loop fusion | flops 4587520 | bytes 18366464 | tf_op jit(solution)/shard_map/while/body/eval_jaxpr/add | solution.py:62
  233.5 5.8 eq.145
  242.3 5.8 mul.382
  248.1 8.7 %select_add_fusion.2 = f32[7,40,4096]{2,1,0:T(8,128)} fusion(f32[7,40,4096]{2,1,0:T(8,128)} %get-tuple-element.151, f32[7,40,4096]{2,1,0:T(8,128)} %mul.382, s32[7,40,4096]{2,1,0:T(8,128)} %eq.145, s32[4096]{0:T(1024)S(1)} %iota_bitcast_fusion.2, pred[]{:T(512)S(6)} %compare.3), kind=kLoop, calls=%fused_computation.clone.1 | loop fusion | flops 4587520 | bytes 18366464 | tf_op jit(solution)/shard_map/while/body/eval_jaxpr/add | solution.py:62
  262.3 5.8 eq.145
  271.0 5.8 mul.382
  276.8 8.7 %select_add_fusion.2 = f32[7,40,4096]{2,1,0:T(8,128)} fusion(f32[7,40,4096]{2,1,0:T(8,128)} %get-tuple-element.151, f32[7,40,4096]{2,1,0:T(8,128)} %mul.382, s32[7,40,4096]{2,1,0:T(8,128)} %eq.145, s32[4096]{0:T(1024)S(1)} %iota_bitcast_fusion.2, pred[]{:T(512)S(6)} %compare.3), kind=kLoop, calls=%fused_computation.clone.1 | loop fusion | flops 4587520 | bytes 18366464 | tf_op jit(solution)/shard_map/while/body/eval_jaxpr/add | solution.py:62
  286.6 4.4 eq.144
  291.0 5.8 eq.145
  299.7 5.8 mul.382
  305.5 8.7 %select_add_fusion.2 = f32[7,40,4096]{2,1,0:T(8,128)} fusion(f32[7,40,4096]{2,1,0:T(8,128)} %get-tuple-element.151, f32[7,40,4096]{2,1,0:T(8,128)} %mul.382, s32[7,40,4096]{2,1,0:T(8,128)} %eq.145, s32[4096]{0:T(1024)S(1)} %iota_bitcast_fusion.2, pred[]{:T(512)S(6)} %compare.3), kind=kLoop, calls=%fused_computation.clone.1 | loop fusion | flops 4587520 | bytes 18366464 | tf_op jit(solution)/shard_map/while/body/eval_jaxpr/add | solution.py:62
  319.7 5.8 eq.145
  328.4 5.8 mul.382
  334.2 8.7 %select_add_fusion.2 = f32[7,40,4096]{2,1,0:T(8,128)} fusion(f32[7,40,4096]{2,1,0:T(8,128)} %get-tuple-element.151, f32[7,40,4096]{2,1,0:T(8,128)} %mul.382, s32[7,40,4096]{2,1,0:T(8,128)} %eq.145, s32[4096]{0:T(1024)S(1)} %iota_bitcast_fusion.2, pred[]{:T(512)S(6)} %compare.3), kind=kLoop, calls=%fused_computation.clone.1 | loop fusion | flops 4587520 | bytes 18366464 | tf_op jit(solution)/shard_map/while/body/eval_jaxpr/add | solution.py:62
  348.4 5.8 eq.145
  357.1 5.8 mul.382
  362.9 8.7 %select_add_fusion.2 = f32[7,40,4096]{2,1,0:T(8,128)} fusion(f32[7,40,4096]{2,1,0:T(8,128)} %get-tuple-element.151, f32[7,40,4096]{2,1,0:T(8,128)} %mul.382, s32[7,40,4096]{2,1,0:T(8,128)} %eq.145, s32[4096]{0:T(1024)S(1)} %iota_bitcast_fusion.2, pred[]{:T(512)S(6)} %compare.3), kind=kLoop, calls=%fused_computation.clone.1 | loop fusion | flops 4587520 | bytes 18366464 | tf_op jit(solution)/shard_map/while/body/eval_jaxpr/add | solution.py:62
  372.7 4.4 eq.144
  377.1 5.8 eq.145
  385.8 5.8 mul.382
  391.6 8.7 %select_add_fusion.2 = f32[7,40,4096]{2,1,0:T(8,128)} fusion(f32[7,40,4096]{2,1,0:T(8,128)} %get-tuple-element.151, f32[7,40,4096]{2,1,0:T(8,128)} %mul.382, s32[7,40,4096]{2,1,0:T(8,128)} %eq.145, s32[4096]{0:T(1024)S(1)} %iota_bitcast_fusion.2, pred[]{:T(512)S(6)} %compare.3), kind=kLoop, calls=%fused_computation.clone.1 | loop fusion | flops 4587520 | bytes 18366464 | tf_op jit(solution)/shard_map/while/body/eval_jaxpr/add | solution.py:62
  400.4 8.3 %reshape.99 = f32[7,40,64,64]{3,2,1,0:T(8,128)} reshape(f32[7,40,4096]{2,1,0:T(8,128)} %get-tuple-element.81) | data formatting | bytes 9175040 | tf_op jit(solution)/shard_map/reshape | solution.py:30
  408.7 11.8 %fusion.26 = f32[7,40,64,64]{2,3,1,0:T(8,128)S(1)} fusion(f32[7,40,64,64]{3,2,1,0:T(8,128)} %reshape.99, f32[64]{0:T(128)S(1)} %get-tuple-element.117, f32[64]{0:T(128)S(1)} %get-tuple-element.118), kind=kOutput, calls=%fused_computation.44 | convolution fusion | flops 880816128 | bytes 9175552 | tf_op jit(solution)/shard_map/ak,xyab,bl->xkyl/dot_general | solution.py:31
  420.5 11.5 %multiply_bitcast_fusion = f32[7,64,40,64]{3,1,2,0:T(8,128)S(1)} fusion(f32[7,40,64,64]{2,3,1,0:T(8,128)S(1)} %fusion.26, f32[64]{0:T(128)S(1)} %get-tuple-element.117, f32[64]{0:T(128)S(1)} %get-tuple-element.118), kind=kOutput, calls=%fused_computation.13 | convolution fusion | flops 881963008 | bytes 9175552 | tf_op jit(solution)/shard_map/ak,xyab,bl->xkyl/dot_general | solution.py:31
  432.0 8.7 %copy.29 = f32[7,64,40,64]{3,2,1,0:T(8,128)} copy(f32[7,64,40,64]{3,1,2,0:T(8,128)S(1)} %multiply_bitcast_fusion) | data formatting | bytes 9175040 | tf_op jit(solution)/shard_map/mul | solution.py:99
  440.7 8.4 %mul.223 = f32[448,2560]{1,0:T(8,128)} reshape(f32[7,64,40,64]{3,2,1,0:T(8,128)} %copy.29) | data formatting | bytes 9175040 | tf_op jit(solution)/shard_map/mul | solution.py:99
  449.1 48.3 %all-gather.1 = bf16[32,80,64]{1,2,0:T(8,128)(2,1)S(1)} all-gather(bf16[1,80,64]{1,2,0:T(8,128)(2,1)S(1)} %bitcast.75), channel_id=1, replica_groups=mesh['replica'=8,'tensor'=32] {'tensor'}, dimensions={0}, use_global_device_ids=true | all-gather | bytes 337920 | tf_op jit(solution)/shard_map/all_gather | solution.py:80
  501.0 5.2 convolution_convert_fusion
  506.5 26.7 %fusion.1 = f32[7,40,64,64]{2,3,1,0:T(8,128)S(1)} fusion(f32[7,40,64]{2,1,0:T(8,128)S(1)} %copy.30, s32[64,64]{0,1:T(8,128)S(1)} %copy.22, s32[7,40,64]{2,1,0:T(8,128)S(1)} %copy.21, f32[64]{0:T(128)S(1)} %get-tuple-element.117, f32[64]{0:T(128)S(1)} %get-tuple-element.118), kind=kOutput, calls=%fused_computation.10 | convolution fusion | flops 883109888 | bytes 4747776 | tf_op jit(solution)/shard_map/ak,xyab,bl->xkyl/dot_general | solution.py:31
  533.2 11.7 %convolution_bitcast_fusion = f32[7,64,40,64]{3,1,2,0:T(8,128)S(1)} fusion(f32[7,40,64,64]{2,3,1,0:T(8,128)S(1)} %fusion.1, f32[64]{0:T(128)S(1)} %get-tuple-element.117, f32[64]{0:T(128)S(1)} %get-tuple-element.118), kind=kOutput, calls=%fused_computation.22 | convolution fusion | flops 880816128 | bytes 9175552 | tf_op jit(solution)/shard_map/ak,xyab,bl->xkyl/dot_general | solution.py:31
  544.9 8.7 %copy.32 = f32[7,64,40,64]{3,2,1,0:T(8,128)} copy(f32[7,64,40,64]{3,1,2,0:T(8,128)S(1)} %convolution_bitcast_fusion) | data formatting | bytes 9175040 | tf_op jit(solution)/shard_map/ak,xyab,bl->xkyl/transpose | solution.py:31
  553.5 8.4 %reshape.100 = f32[448,2560]{1,0:T(8,128)} reshape(f32[7,64,40,64]{3,2,1,0:T(8,128)} %copy.32) | data formatting | bytes 9175040 | tf_op jit(solution)/shard_map/reshape | solution.py:32
  561.9 5.7 fusion.8
  568.9 79.3 %all-reduce.3.cloned.1.call-done = bf16[64,2560]{1,0:T(8,128)(2,1)} async-done(((bf16[64,2560]{1,0:T(8,128)(2,1)}), bf16[64,2560]{1,0:T(8,128)(2,1)}) %all-reduce.3.cloned.1.call-update) | async-done | bytes 327696
  (104 shorter events, 63.4 us)
Async XLA Ops:
  7.2 106.7 %copy-start = (bf16[2560,448]{0,1:T(8,128)(2,1)S(1)}, bf16[2560,448]{0,1:T(8,128)(2,1)}, u32[]{:S(2)}) copy-start(bf16[2560,448]{0,1:T(8,128)(2,1)} %param.14) | copy-start | bytes 6881284
  7.2 641.1 %all-reduce.3.cloned.1.call-start = ((), (), s32[]{:S(2)}) async-start(), calls=%async_computation | async-start | bytes 655360
  440.7 8.4 %copy-start.1 = (bf16[64,80]{1,0:T(8,128)(2,1)S(1)}, bf16[64,80]{1,0:T(8,128)(2,1)}, u32[]{:S(2)}) copy-start(bf16[64,80]{1,0:T(8,128)(2,1)} %param.11) | copy-start | bytes 30724
  561.9 5.7 copy-start.2
Sparse Core Ops, SparseCore 0:
  506.4 141.7 all-reduce.2
where the time goes:
time: 664 us; the launch traced here: 657 us
  local copies, waits for them, and re-layouts  213 us (32%)
  blocking collectives  166 us (25%)
  matrix products  106 us (16%)
  waiting for transfers between devices  79.4 us (12%)
  other arithmetic  75.9 us (11%)
  between operations  15.1 us (2%)
    eq x28, local copies, waits for them, and re-layouts, one_hot_slots(): return (offset[..., None] == slots).astype(jnp.float32)  81.6 us
    unnamed x2, waiting for transfers between devices  79.4 us
    mul x18, local copies, waits for them, and re-layouts, place_values(): placed = values[..., None] * one_hot_slots(where)  69.1 us
    add x8, other arithmetic, add_replica(): return dense + place_values(values, spots)  68.6 us
    dot_general x4, matrix products, inverse_tiles(): jnp.einsum('ak,xyab,bl->xkyl', table, blocks, table, precision=lax.Precis...  61.6 us
    all_gather x1, blocking collectives, on_device(): lax.all_gather(cotangent, 'tensor', axis=1, tiled=True)  52.1 us
    all_gather x1, blocking collectives, on_device(): lax.all_gather(tokens, 'tensor', axis=1, tiled=True)  52 us
    all_gather x1, blocking collectives, on_device(): lax.all_gather(next_tokens, 'tensor', axis=1, tiled=True)  48.3 us
  transfers between devices with their start and end apart: 1, of which 1 were waited for; matrix products, arithmetic and copies ran while one was open for 9% of the time, Pallas kernels for 0%

commit v1 on v0

v1 whole, which is shorter than its diff:
```python
import functools

import jax
import jax.numpy as jnp
import ml_dtypes
import numpy as np
from jax import lax
from jax.experimental import pallas as pl
from jax.experimental.pallas import tpu as pltpu
from jax.sharding import PartitionSpec as P

TILE = 64
BETA_DECAY = 0.9
STEP_RATE = 0.1
BAND = 256
HALF = 256
VMEM = pl.BlockSpec(memory_space=pltpu.VMEM)
F32 = jnp.float32
BF16 = jnp.bfloat16


def cosine_table():
    freq = np.arange(TILE, dtype=np.float64)[:, None]
    place = np.arange(TILE, dtype=np.float64)[None, :]
    table = np.cos(np.pi * (2.0 * place + 1.0) * freq / (2.0 * TILE))
    return table * np.where(freq == 0.0, np.sqrt(1.0 / TILE), np.sqrt(2.0 / TILE))


def parts(table):
    high = table.astype(np.float32).astype(ml_dtypes.bfloat16)
    low = (table - high.astype(np.float64)).astype(np.float32).astype(ml_dtypes.bfloat16)
    return high, low


def row_table(rows):
    cosine = cosine_table()
    table = np.zeros((rows, 2 * HALF))
    for i in range(rows // TILE):
        for p in range(2):
            lanes = slice(p * HALF + i * (TILE // 2), p * HALF + (i + 1) * (TILE // 2))
            table[i * TILE : (i + 1) * TILE, lanes] = cosine[p::2].T
    return table


def band_table():
    return np.kron(np.eye(BAND // TILE), cosine_table())


def split(value):
    high = value.astype(BF16)
    return high, (value - high.astype(F32)).astype(BF16)


def dot(a, b):
    return jnp.dot(a, b, preferred_element_type=F32)


def dot3(a, b):
    return dot(a[0], b[0]) + (dot(a[1], b[0]) + dot(a[0], b[1]))


def momentum_spectrum_kernel(momentum, rows_high, rows_low, band_high, band_low, out):
    turned = momentum[0].T
    along = split(dot(turned, rows_high[...]) + dot(turned, rows_low[...]))
    out[...] = dot3((band_high[...], band_low[...]), along)


def spread(offsets, values, tile):
    column = lax.broadcasted_iota(jnp.int32, (TILE, HALF), 0)
    even = jnp.where(offsets == column, values, 0.0)
    odd = jnp.where(offsets == column + TILE, values, 0.0)
    return even, odd


def pick_kernel(cotangent, hidden_high, hidden_low, band_high, band_low, spectrum, offsets, out):
    turned = cotangent[...]
    grads = split(dot(band_high[...], turned) + dot(band_low[...], turned))
    whole = spectrum[...] + dot3(grads, (hidden_high[...], hidden_low[...]))
    column = lax.broadcasted_iota(jnp.int32, (TILE, HALF), 0)
    step = pl.program_id(0)
    tiles = BAND // TILE
    for k in range(tiles):
        spots = offsets[pl.ds(step * tiles + k, 1), :]
        even = whole[k * TILE : (k + 1) * TILE, :HALF]
        odd = whole[k * TILE : (k + 1) * TILE, HALF:]
        hit = jnp.where(spots == column, even, jnp.where(spots == column + TILE, odd, 0.0))
        out[pl.ds(step * tiles + k, 1), :] = jnp.sum(hit, axis=0, keepdims=True)


def output_kernel(values, offsets, next_rows, base, back_high, back_low, out, dense, listed):
    step = pl.program_id(0)
    tiles = BAND // TILE
    replicas = values.shape[0]

    @pl.when(step == 0)
    def _():
        listed[...] = values[...].astype(F32)

    column = lax.broadcasted_iota(jnp.int32, (TILE, HALF), 0)
    for k in range(tiles):
        even = jnp.zeros((TILE, HALF), F32)
        odd = jnp.zeros((TILE, HALF), F32)
        for r in range(replicas):
            spots = offsets[r, pl.ds(step * tiles + k, 1), :]
            value = listed[r, pl.ds(step * tiles + k, 1), :]
            even += jnp.where(spots == column, value, 0.0)
            odd += jnp.where(spots == column + TILE, value, 0.0)
        dense[k * TILE : (k + 1) * TILE, :HALF] = even.astype(BF16)
        dense[k * TILE : (k + 1) * TILE, HALF:] = odd.astype(BF16)
    both = dot(dense[...], next_rows[...])
    tokens = both.shape[1] // 2
    folded = both[:, :tokens] + both[:, tokens:]
    change = dot3((back_high[...], back_low[...]), split(folded))
    out[...] = (base[...] - (STEP_RATE / replicas) * change.T).astype(BF16)


def kept_kernel(sent, offsets, cotangent, hidden, momentum, back_high, back_low, rows_high, rows_low, out, dense):
    step = pl.program_id(0)
    tiles = BAND // TILE
    column = lax.broadcasted_iota(jnp.int32, (TILE, HALF), 0)
    for k in range(tiles):
        spots = offsets[pl.ds(step * tiles + k, 1), :]
        value = sent[pl.ds(step * tiles + k, 1), :]
        dense[k * TILE : (k + 1) * TILE, :HALF] = jnp.where(spots == column, value, 0.0).astype(BF16)
        dense[k * TILE : (k + 1) * TILE, HALF:] = jnp.where(spots == column + TILE, value, 0.0).astype(BF16)
    own = dense[...]
    along = split(dot(back_high[...], own) + dot(back_low[...], own))
    change = dot(cotangent[...], hidden[...]) - dot3(along, (rows_high[...], rows_low[...]))
    out[0] = (BETA_DECAY * momentum[0].astype(F32) + change.T).astype(BF16)


def whole_block(shape):
    return pl.BlockSpec(shape, lambda step: (0,) * len(shape))


def params():
    return pltpu.CompilerParams(dimension_semantics=("arbitrary",), vmem_limit_bytes=32 * 1024 * 1024)


def gather_rows(block, count):
    blocks = jnp.broadcast_to(block[None], (count,) + block.shape)
    return lax.all_to_all(blocks, "tensor", 0, 0, tiled=True).reshape(-1, block.shape[1])


def project(turned, weight):
    return lax.dot_general(turned, weight, (((0,), (0,)), ((), ())), preferred_element_type=F32)


def swiglu(turned, gate_weight, up_weight):
    return (jax.nn.silu(project(turned, gate_weight)) * project(turned, up_weight)).astype(BF16)


def on_device(tokens, next_tokens, cotangent, gate_weight, up_weight, down_weight, momentum, indices):
    shards = lax.axis_size("tensor")
    replicas = lax.axis_size("replica")
    replica = lax.axis_index("replica")
    rows, width = down_weight.shape
    bands = width // BAND
    tile_rows, tile_cols, keep = indices.shape[1:]
    stride = TILE * TILE // keep

    table = row_table(rows)
    rows_high, rows_low = parts(table)
    decayed_high, decayed_low = parts(BETA_DECAY * table)
    rows_back_high, rows_back_low = parts(table.T)
    band_high, band_low = parts(band_table())
    back_high, back_low = parts(band_table().T)

    offsets = indices - jnp.arange(keep, dtype=jnp.int32) * stride
    offsets = offsets.transpose(0, 2, 1, 3).reshape(replicas, tile_cols, tile_rows * keep)
    offsets = jnp.pad(offsets, ((0, 0), (0, 0), (0, HALF - tile_rows * keep)), constant_values=-1)
    own_offsets = lax.dynamic_index_in_dim(offsets, replica, 0, keepdims=False)

    count = tokens.shape[0]
    momentum_spectrum = pl.pallas_call(
        momentum_spectrum_kernel,
        grid=(bands,),
        in_specs=[pl.BlockSpec((1, rows, BAND), lambda step: (0, 0, step))]
        + [whole_block((rows, 2 * HALF))] * 2
        + [whole_block((BAND, BAND))] * 2,
        out_specs=pl.BlockSpec((BAND, 2 * HALF), lambda step: (step, 0)),
        out_shape=jax.ShapeDtypeStruct((width, 2 * HALF), F32),
        compiler_params=params(),
        cost_estimate=pl.CostEstimate(flops=9_000_000_000, bytes_accessed=8_000_000, transcendentals=0),
        name="momentum_spectrum",
    )(momentum, decayed_high, decayed_low, band_high, band_low)

    whole = gather_rows(tokens.T, shards)
    whole_grads = gather_rows(cotangent.T, shards)
    whole_next = gather_rows(next_tokens.T, shards)

    hidden = swiglu(whole, gate_weight, up_weight)
    hidden_high, hidden_low = split(dot(hidden, rows_high) + dot(hidden, rows_low))

    sent = pl.pallas_call(
        pick_kernel,
        grid=(bands,),
        in_specs=[pl.BlockSpec((BAND, count), lambda step: (step, 0))]
        + [whole_block((count, 2 * HALF))] * 2
        + [whole_block((BAND, BAND))] * 2
        + [pl.BlockSpec((BAND, 2 * HALF), lambda step: (step, 0)), whole_block((tile_cols, HALF))],
        out_specs=whole_block((tile_cols, HALF)),
        out_shape=jax.ShapeDtypeStruct((tile_cols, HALF), F32),
        compiler_params=params(),
        cost_estimate=pl.CostEstimate(flops=2_000_000_000, bytes_accessed=6_000_000, transcendentals=0),
        name="pick",
    )(whole_grads, hidden_high, hidden_low, band_high, band_low, momentum_spectrum, own_offsets)
    sent = sent.astype(BF16)

    listed = lax.all_to_all(
        jnp.broadcast_to(sent.reshape(-1, 128)[None], (replicas, sent.size // 128, 128)), "replica", 0, 0, tiled=True
    ).reshape(replicas, tile_cols, HALF)

    next_hidden = swiglu(whole_next, gate_weight, up_weight)
    base = dot(next_hidden, down_weight)
    next_rows = jnp.concatenate(split((dot(next_hidden, rows_high) + dot(next_hidden, rows_low)).T), axis=1)
    next_count = next_tokens.shape[0]

    partial = pl.pallas_call(
        output_kernel,
        grid=(bands,),
        in_specs=[
            whole_block((replicas, tile_cols, HALF)),
            whole_block((replicas, tile_cols, HALF)),
            whole_block((2 * HALF, 2 * next_count)),
            pl.BlockSpec((next_count, BAND), lambda step: (0, step)),
            whole_block((BAND, BAND)),
            whole_block((BAND, BAND)),
        ],
        out_specs=pl.BlockSpec((next_count, BAND), lambda step: (0, step)),
        out_shape=jax.ShapeDtypeStruct((next_count, width), BF16),
        scratch_shapes=[pltpu.VMEM((BAND, 2 * HALF), BF16), pltpu.VMEM((replicas, tile_cols, HALF), F32)],
        compiler_params=params(),
        cost_estimate=pl.CostEstimate(flops=3_000_000_000, bytes_accessed=2_000_000, transcendentals=0),
        name="output_part",
    )(listed, offsets, next_rows, base, back_high, back_low)

    pieces = lax.all_to_all(partial.reshape(shards, -1, 128), "tensor", 0, 0, tiled=True)
    output = jnp.sum(pieces.astype(F32), axis=0).astype(BF16).reshape(next_count // shards, width)

    kept = pl.pallas_call(
        kept_kernel,
        grid=(bands,),
        in_specs=[
            whole_block((tile_cols, HALF)),
            whole_block((tile_cols, HALF)),
            pl.BlockSpec((BAND, count), lambda step: (step, 0)),
            whole_block((count, rows)),
            pl.BlockSpec((1, rows, BAND), lambda step: (0, 0, step)),
            whole_block((BAND, BAND)),
            whole_block((BAND, BAND)),
            whole_block((2 * HALF, rows)),
            whole_block((2 * HALF, rows)),
        ],
        out_specs=pl.BlockSpec((1, rows, BAND), lambda step: (0, 0, step)),
        out_shape=jax.ShapeDtypeStruct((1, rows, width), BF16),
        scratch_shapes=[pltpu.VMEM((BAND, 2 * HALF), BF16)],
        compiler_params=params(),
        cost_estimate=pl.CostEstimate(flops=12_000_000_000, bytes_accessed=8_000_000, transcendentals=0),
        name="kept",
    )(sent.astype(F32), own_offsets, whole_grads, hidden, momentum, back_high, back_low, rows_back_high, rows_back_low)
    return (output, kept)


def solution(mesh):
    return jax.shard_map(
        on_device,
        mesh=mesh,
        in_specs=(
            P("replica", "tensor"),
            P("replica", "tensor"),
            P("replica", "tensor"),
            P(None, "tensor"),
            P(None, "tensor"),
            P("tensor", None),
            P("replica", "tensor", None),
            P(None, "tensor", None, None),
        ),
        out_specs=(P(("replica", "tensor"), None), P("replica", "tensor", None)),
        check_vma=False,
    )
```

time: 664 us -> 148 us (0.22)
  local copies, waits for them, and re-layouts: 213 us -> 36.4 us
  blocking collectives: 166 us -> 0 us
  matrix products: 106 us -> 9.72 us
  other arithmetic: 75.9 us -> 3.13 us
  waiting for transfers between devices: 79.4 us -> 28.5 us
  starting transfers between devices: 0.04 us -> 33.9 us
  Pallas kernels: 0 us -> 33.2 us
  between operations: 15.1 us -> 0.96 us
    all_gather x4 -> x0, blocking collectives: 166 us -> none  [the longest x1 52.1 us: on_device(): lax.all_gather(cotangent, 'tensor', axis=1, tiled=True)]
    dot_general x10 -> x9, matrix products: 106 us -> 9.72 us  [the longest x4 7.49 us: project(): lax.dot_general(turned, weight, (((0,), (0,)), ((), ())), preferred_eleme...]
    mul x20 -> x0, local copies, waits for them, and re-layouts: 86.2 us -> none  [the longest x18 69.1 us: place_values(): placed = values[..., None] * one_hot_slots(where)]
    eq x28 -> x0, local copies, waits for them, and re-layouts: 81.6 us -> none  [one_hot_slots(): return (offset[..., None] == slots).astype(jnp.float32)]
    unnamed x2 -> x0, waiting for transfers between devices: 79.4 us -> none
    add x8 -> x0, other arithmetic: 68.6 us -> none  [add_replica(): return dense + place_values(values, spots)]
    all_to_all x0 -> x5, starting transfers between devices: none -> 33.9 us  [the longest x3 24.4 us: gather_rows(): lax.all_to_all(blocks, 'tensor', 0, 0, tiled=True)]
    pallas_call x0 -> x4, Pallas kernels: none -> 33.2 us  [the longest x1 10.3 us: on_device(): pl.pallas_call(kept_kernel, grid=(bands,), in_specs=[whole_block((tile_co...]
  transfers between devices with their start and end apart: 1 -> 5, of which waited for: 1 -> 4; matrix products, arithmetic and copies ran while one was open for 9% -> 12% of each run, Pallas kernels for 0% -> 13%
where the time goes in v1:
time: 148 us; the launch traced here: 146 us
  local copies, waits for them, and re-layouts  36.4 us (25%)
  starting transfers between devices  33.9 us (23%)
  Pallas kernels  33.2 us (22%)
  waiting for transfers between devices  28.5 us (19%)
  matrix products  9.72 us (7%)
  other arithmetic  3.13 us (2%)
    all_to_all x3, starting transfers between devices, gather_rows(): lax.all_to_all(blocks, 'tensor', 0, 0, tiled=True)  24.4 us
    unnamed x66, local copies, waits for them, and re-layouts  23.6 us
    all_to_all x3, waiting for transfers between devices, gather_rows(): lax.all_to_all(blocks, 'tensor', 0, 0, tiled=True)  23.1 us
    pallas_call x1, Pallas kernels, on_device(): pl.pallas_call(kept_kernel, grid=(bands,), in_specs=[whole_block((tile_co...  10.3 us
    pallas_call x1, Pallas kernels, on_device(): pl.pallas_call(output_kernel, grid=(bands,), in_specs=[whole_block((repli...  9.5 us
    pallas_call x1, Pallas kernels, on_device(): pl.pallas_call(momentum_spectrum_kernel, grid=(bands,), in_specs=[pl.Bloc...  8.22 us
    dot_general x4, matrix products, project(): lax.dot_general(turned, weight, (((0,), (0,)), ((), ())), preferred_eleme...  7.49 us
    all_to_all x1, waiting for transfers between devices, on_device(): lax.all_to_all(jnp.broadcast_to(sent.reshape(-1, 128)[None], (replicas, s...  5.38 us
  transfers between devices with their start and end apart: 5, of which 4 were waited for; matrix products, arithmetic and copies ran while one was open for 12% of the time, Pallas kernels for 13%

profile of v1, /device:TPU:32, one launch (start us, length us, event | category | flops | bytes accessed | tf_op | source)
XLA Modules:
  0.0 145.8 jit_solution(7178117463077570823)
XLA Ops:
  0.6 1.8 %broadcast_in_dim.14 = bf16[32,80,64]{1,2,0:T(8,128)(2,1)} broadcast(bf16[80,64]{0,1:T(8,128)(2,1)} %bitcast.41), dimensions={1,2} | broadcast | bytes 337920 | tf_op jit(solution)/shard_map/broadcast_in_dim | solution.py:141
  2.4 11.2 %all-to-all-start.3 = ((bf16[32,80,64]{1,2,0:T(8,128)(2,1)}), bf16[32,80,64]{1,2,0:T(8,128)(2,1)S(1)}, u32[]{:S(2)}, u32[]{:S(2)}) async-start(bf16[32,80,64]{1,2,0:T(8,128)(2,1)} %broadcast_in_dim.14), calls=%async_computation.3 | async-start | bytes 1048576 | tf_op jit(solution)/shard_map/all_to_all | solution.py:142
  13.6 1.6 %copy-done.7 = bf16[1,448,2560]{2,1,0:T(8,128)(2,1)S(1)} copy-done((bf16[1,448,2560]{2,1,0:T(8,128)(2,1)S(1)}, bf16[1,448,2560]{2,1,0:T(8,128)(2,1)}, u32[]{:S(2)}) %copy-start.7) | copy-done | bytes 2293784
  15.3 1.0 copy-done.11
  16.3 1.0 copy-done.12
  17.3 0.9 copy-done.17
  18.2 0.9 copy-done.19
  19.1 8.2 %momentum_spectrum.1.spectrum = f32[2560,512]{1,0:T(8,128)S(1)} custom-call(bf16[1,448,2560]{2,1,0:T(8,128)(2,1)S(1)} %copy-done.7, bf16[448,512]{1,0:T(8,128)(2,1)S(1)} %copy-done.11, bf16[448,512]{1,0:T(8,128)(2,1)S(1)} %copy-done.12, bf16[256,256]{1,0:T(8,128)(2,1)S(1)} %copy-done.17, bf16[256,256]{1,0:T(8,128)(2,1)S(1)} %copy-done.19), custom_call_target="tpu_custom_call" | custom-call | flops 8999999488 | bytes 8000000 | tf_op jit(solution)/shard_map/momentum_spectrum/pallas_call | solution.py:175
  27.4 2.3 %copy-done.21 = f32[2560,512]{1,0:T(8,128)} copy-done((f32[2560,512]{1,0:T(8,128)}, f32[2560,512]{1,0:T(8,128)S(1)}, u32[]{:S(2)}) %copy-start.21) | copy-done | bytes 5242904
  29.7 1.6 %all-to-all-done.3 = bf16[32,80,64]{1,2,0:T(8,128)(2,1)S(1)} async-done(((bf16[32,80,64]{1,2,0:T(8,128)(2,1)}), bf16[32,80,64]{1,2,0:T(8,128)(2,1)S(1)}, u32[]{:S(2)}, u32[]{:S(2)}) %all-to-all-start.3) | async-done | bytes 327712 | tf_op jit(solution)/shard_map/all_to_all | solution.py:142
  31.2 1.0 broadcast_in_dim.11
  32.2 8.3 %all-to-all-start.1 = ((bf16[32,80,128]{2,1,0:T(8,128)(2,1)}), bf16[32,80,128]{2,1,0:T(8,128)(2,1)}, u32[]{:S(2)}, u32[]{:S(2)}) async-start(bf16[32,80,128]{2,1,0:T(8,128)(2,1)} %broadcast_in_dim.11), calls=%async_computation.1 | async-start | bytes 1310720 | tf_op jit(solution)/shard_map/all_to_all | solution.py:142
  40.5 1.4 broadcast_subtract_fusion
  42.2 0.7 pad.4.offsets
  43.0 2.2 %copy.51 = bf16[32,80,64]{1,0,2:T(8,128)(2,1)} copy(bf16[32,80,64]{1,2,0:T(8,128)(2,1)} %copy-done.26) | data formatting | bytes 655360 | tf_op jit(solution)/shard_map/all_to_all | solution.py:142
  45.2 1.8 %reshape.37 = bf16[2560,64]{0,1:T(8,128)(2,1)S(1)} reshape(bf16[32,80,64]{1,0,2:T(8,128)(2,1)} %copy.51) | data formatting | bytes 655360 | tf_op jit(solution)/shard_map/reshape | solution.py:142
  47.0 2.6 %fusion.6 = f32[64,448]{1,0:T(8,128)S(1)} fusion(bf16[2560,64]{0,1:T(8,128)(2,1)S(1)} %reshape.37, bf16[2560,448]{0,1:T(8,128)(2,1)} %param.21), kind=kOutput, calls=%fused_computation.17 | convolution fusion | flops 146800640 | bytes 2736128 | tf_op jit(solution)/shard_map/dot_general | solution.py:146
  49.6 0.8 fusion.1
  50.8 0.8 copy.52
  51.6 8.7 %all-to-all-done.1 = bf16[32,80,128]{2,1,0:T(8,128)(2,1)} async-done(((bf16[32,80,128]{2,1,0:T(8,128)(2,1)}), bf16[32,80,128]{2,1,0:T(8,128)(2,1)}, u32[]{:S(2)}, u32[]{:S(2)}) %all-to-all-start.1) | async-done | bytes 655392 | tf_op jit(solution)/shard_map/all_to_all | solution.py:142
  60.4 0.9 broadcast_in_dim.10
  61.3 5.0 %all-to-all-start = ((bf16[32,80,128]{2,1,0:T(8,128)(2,1)}), bf16[32,80,128]{2,1,0:T(8,128)(2,1)S(1)}, u32[]{:S(2)}, u32[]{:S(2)}) async-start(bf16[32,80,128]{2,1,0:T(8,128)(2,1)} %broadcast_in_dim.10), calls=%async_computation | async-start | bytes 1310720 | tf_op jit(solution)/shard_map/all_to_all | solution.py:142
  66.3 1.4 fusion.8.base
  68.2 2.1 %fusion.4 = f32[128,448]{1,0:T(8,128)S(1)} fusion(bf16[2560,128]{1,0:T(8,128)(2,1)} %bitcast.3, bf16[2560,448]{0,1:T(8,128)(2,1)S(1)} %copy-done.23), kind=kOutput, calls=%fused_computation.15 | convolution fusion | flops 293601280 | bytes 3178496 | tf_op jit(solution)/shard_map/dot_general | solution.py:146
  70.3 2.0 %fusion.hidden = bf16[128,448]{1,0:T(8,128)(2,1)S(1)} fusion(bf16[2560,128]{1,0:T(8,128)(2,1)} %bitcast.3, bf16[2560,448]{0,1:T(8,128)(2,1)S(1)} %copy-done.25, f32[128,448]{1,0:T(8,128)S(1)} %fusion.4), kind=kOutput, calls=%fused_computation.2 | convolution fusion | flops 293945344 | bytes 3293184 | tf_op jit(solution)/shard_map/dot_general | solution.py:146
  72.8 12.9 %all-to-all-done = bf16[32,80,128]{2,1,0:T(8,128)(2,1)S(1)} async-done(((bf16[32,80,128]{2,1,0:T(8,128)(2,1)}), bf16[32,80,128]{2,1,0:T(8,128)(2,1)S(1)}, u32[]{:S(2)}, u32[]{:S(2)}) %all-to-all-start) | async-done | bytes 655392 | tf_op jit(solution)/shard_map/all_to_all | solution.py:142
  85.7 0.9 copy-done.20
  86.6 2.5 %copy-done.22 = f32[2560,512]{1,0:T(8,128)S(1)} copy-done((f32[2560,512]{1,0:T(8,128)S(1)}, f32[2560,512]{1,0:T(8,128)}, u32[]{:S(2)}) %copy-start.22) | copy-done | bytes 5242904
  89.1 5.1 %pick.1 = f32[40,256]{1,0:T(8,128)S(1)} custom-call(bf16[2560,128]{1,0:T(8,128)(2,1)S(1)} %bitcast.36, bf16[128,512]{1,0:T(8,128)(2,1)S(1)} %get-tuple-element.7.hidden_high, bf16[128,512]{1,0:T(8,128)(2,1)S(1)} %get-tuple-element.6.hidden_low, bf16[256,256]{1,0:T(8,128)(2,1)S(1)} %copy-done.18, bf16[256,256]{1,0:T(8,128)(2,1)S(1)} %copy-done.20, ...), custom_call_target="tpu_custom_call" | custom-call | flops 2000000000 | bytes 6000000 | tf_op jit(solution)/shard_map/pick/pallas_call | solution.py:195
  95.6 4.5 %all-to-all-start.2 = ((bf16[8,80,128]{2,1,0:T(8,128)(2,1)}), bf16[8,80,128]{2,1,0:T(8,128)(2,1)S(1)}, u32[]{:S(2)}, u32[]{:S(2)}) async-start(bf16[8,80,128]{2,1,0:T(8,128)(2,1)} %broadcast_in_dim.13), calls=%async_computation.2 | async-start | bytes 327680 | tf_op jit(solution)/shard_map/all_to_all | solution.py:210
  100.1 1.0 fusion.2
  101.2 5.4 %all-to-all-done.2 = bf16[8,80,128]{2,1,0:T(8,128)(2,1)S(1)} async-done(((bf16[8,80,128]{2,1,0:T(8,128)(2,1)}), bf16[8,80,128]{2,1,0:T(8,128)(2,1)S(1)}, u32[]{:S(2)}, u32[]{:S(2)}) %all-to-all-start.2) | async-done | bytes 163872 | tf_op jit(solution)/shard_map/all_to_all | solution.py:210
  107.3 1.1 copy-done.1
  108.4 1.0 copy-done.2
  109.3 0.9 copy-done.3
  110.2 0.9 copy-done.13
  111.1 0.9 copy-done.15
  112.0 9.5 %output_part.1 = bf16[64,2560]{1,0:T(8,128)(2,1)S(1)} custom-call(bf16[8,40,256]{2,1,0:T(8,128)(2,1)S(1)} %copy-done.3, s32[8,40,256]{2,1,0:T(8,128)S(1)} %copy-done.2, bf16[512,128]{1,0:T(8,128)(2,1)S(1)} %pad_maximum_fusion.next_rows, f32[64,2560]{1,0:T(8,128)S(1)} %copy-done.1, bf16[256,256]{1,0:T(8,128)(2,1)S(1)} %copy-done.13, ...), custom_call_target="tpu_custom_call" | custom-call | flops 3000000000 | bytes 2000000 | tf_op jit(solution)/shard_map/output_part/pallas_call | solution.py:219
  121.6 1.1 reshape.38
  122.7 5.0 %all-to-all-start.4 = ((bf16[32,40,128]{2,1,0:T(8,128)(2,1)}), bf16[32,40,128]{2,1,0:T(8,128)(2,1)S(1)}, u32[]{:S(2)}, u32[]{:S(2)}) async-start(bf16[32,40,128]{2,1,0:T(8,128)(2,1)} %reshape.38), calls=%async_computation.4 | async-start | bytes 655360 | tf_op jit(solution)/shard_map/all_to_all | solution.py:238
  127.7 0.8 copy-done.4
  128.5 0.8 copy-done.6
  129.3 1.6 %copy-done.8 = bf16[1,448,2560]{2,1,0:T(8,128)(2,1)S(1)} copy-done((bf16[1,448,2560]{2,1,0:T(8,128)(2,1)S(1)}, bf16[1,448,2560]{2,1,0:T(8,128)(2,1)}, u32[]{:S(2)}) %copy-start.8) | copy-done | bytes 2293784
  130.9 1.0 copy-done.9
  132.0 1.0 copy-done.10
  133.0 0.9 copy-done.14
  133.9 0.9 copy-done.16
  134.8 10.3 %kept.1 = bf16[1,448,2560]{2,1,0:T(8,128)(2,1)} custom-call(f32[40,256]{1,0:T(8,128)S(1)} %copy-done.4, s32[40,256]{1,0:T(8,128)S(1)} %copy-done.6, bf16[2560,128]{1,0:T(8,128)(2,1)S(1)} %bitcast.37, bf16[128,448]{1,0:T(8,128)(2,1)S(1)} %fusion.hidden, bf16[1,448,2560]{2,1,0:T(8,128)(2,1)S(1)} %copy-done.8, bf16[256,256]{1,0:T(8,128)(2,1)S(1)} %copy-done.14, ...), custom_call_target="tpu_custom_call" | custom-call | flops 12000000000 | bytes 8000000 | tf_op jit(solution)/shard_map/kept/pallas_call | solution.py:241
  (61 shorter events, 4.6 us)
Async XLA Ops:
  0.6 65.6 %copy-start = (bf16[448,2560]{1,0:T(8,128)(2,1)S(1)}, bf16[448,2560]{1,0:T(8,128)(2,1)}, u32[]{:S(2)}) copy-start(bf16[448,2560]{1,0:T(8,128)(2,1)} %param.23) | copy-start | bytes 6881284
  2.4 28.8 %all-to-all-start.3 = ((bf16[32,80,64]{1,2,0:T(8,128)(2,1)}), bf16[32,80,64]{1,2,0:T(8,128)(2,1)S(1)}, u32[]{:S(2)}, u32[]{:S(2)}) async-start(bf16[32,80,64]{1,2,0:T(8,128)(2,1)} %broadcast_in_dim.14), calls=%async_computation.3 | async-start | bytes 1048576 | tf_op jit(solution)/shard_map/all_to_all | solution.py:142
  13.6 1.6 %copy-start.7 = (bf16[1,448,2560]{2,1,0:T(8,128)(2,1)S(1)}, bf16[1,448,2560]{2,1,0:T(8,128)(2,1)}, u32[]{:S(2)}) copy-start(bf16[1,448,2560]{2,1,0:T(8,128)(2,1)} %momentum.3) | copy-start | bytes 6881284
  15.3 1.0 copy-start.11
  16.3 1.0 copy-start.12
  17.3 0.9 copy-start.17
  18.2 0.9 copy-start.19
  19.1 12.1 %copy-start.31 = (bf16[128,80]{0,1:T(8,128)(2,1)S(1)}, bf16[128,80]{0,1:T(8,128)(2,1)}, u32[]{:S(2)}) copy-start(bf16[128,80]{0,1:T(8,128)(2,1)} %param.18) | copy-start | bytes 61444
  27.4 2.3 %copy-start.21 = (f32[2560,512]{1,0:T(8,128)}, f32[2560,512]{1,0:T(8,128)S(1)}, u32[]{:S(2)}) copy-start(f32[2560,512]{1,0:T(8,128)S(1)} %momentum_spectrum.1.spectrum) | copy-start | bytes 15728644
  31.2 1.0 copy-start.26
  32.2 28.1 %all-to-all-start.1 = ((bf16[32,80,128]{2,1,0:T(8,128)(2,1)}), bf16[32,80,128]{2,1,0:T(8,128)(2,1)}, u32[]{:S(2)}, u32[]{:S(2)}) async-start(bf16[32,80,128]{2,1,0:T(8,128)(2,1)} %broadcast_in_dim.11), calls=%async_computation.1 | async-start | bytes 1310720 | tf_op jit(solution)/shard_map/all_to_all | solution.py:142
  43.0 42.8 %copy-start.5 = (s32[40,256]{1,0:T(8,128)}, s32[40,256]{1,0:T(8,128)S(1)}, u32[]{:S(2)}) copy-start(s32[40,256]{1,0:T(8,128)S(1)} %dynamic-slice_bitcast_fusion.offsets) | copy-start | bytes 122884
  46.9 2.6 %copy-start.24 = (bf16[2560,448]{0,1:T(8,128)(2,1)S(1)}, bf16[2560,448]{0,1:T(8,128)(2,1)}, u32[]{:S(2)}) copy-start(bf16[2560,448]{0,1:T(8,128)(2,1)} %param.22) | copy-start | bytes 6881284
  46.9 3.4 %copy-start.27 = (bf16[448,512]{1,0:T(8,128)(2,1)S(1)}, bf16[448,512]{1,0:T(8,128)(2,1)}, u32[]{:S(2)}) copy-start(bf16[448,512]{1,0:T(8,128)(2,1)} %constant.48.clone) | copy-start | bytes 1376260
  49.6 1.0 copy-start.29
  49.6 10.8 %copy-start.32 = (bf16[128,80]{0,1:T(8,128)(2,1)S(1)}, bf16[128,80]{0,1:T(8,128)(2,1)}, u32[]{:S(2)}) copy-start(bf16[128,80]{0,1:T(8,128)(2,1)} %param.20) | copy-start | bytes 61444
  61.3 24.4 %all-to-all-start = ((bf16[32,80,128]{2,1,0:T(8,128)(2,1)}), bf16[32,80,128]{2,1,0:T(8,128)(2,1)S(1)}, u32[]{:S(2)}, u32[]{:S(2)}) async-start(bf16[32,80,128]{2,1,0:T(8,128)(2,1)} %broadcast_in_dim.10), calls=%async_computation | async-start | bytes 1310720 | tf_op jit(solution)/shard_map/all_to_all | solution.py:142
  66.3 1.9 %copy-start.23 = (bf16[2560,448]{0,1:T(8,128)(2,1)S(1)}, bf16[2560,448]{0,1:T(8,128)(2,1)}, u32[]{:S(2)}) copy-start(bf16[2560,448]{0,1:T(8,128)(2,1)} %param.21) | copy-start | bytes 6881284
  67.7 2.6 %copy-start.25 = (bf16[2560,448]{0,1:T(8,128)(2,1)S(1)}, bf16[2560,448]{0,1:T(8,128)(2,1)}, u32[]{:S(2)}) copy-start(bf16[2560,448]{0,1:T(8,128)(2,1)} %param.22) | copy-start | bytes 6881284
  70.3 2.1 %copy-start.28 = (bf16[448,512]{1,0:T(8,128)(2,1)S(1)}, bf16[448,512]{1,0:T(8,128)(2,1)}, u32[]{:S(2)}) copy-start(bf16[448,512]{1,0:T(8,128)(2,1)} %constant.48.clone) | copy-start | bytes 1376260
  70.3 2.3 %copy-start.30 = (bf16[448,512]{1,0:T(8,128)(2,1)S(1)}, bf16[448,512]{1,0:T(8,128)(2,1)}, u32[]{:S(2)}) copy-start(bf16[448,512]{1,0:T(8,128)(2,1)} %constant.49.clone) | copy-start | bytes 1376260
  70.3 15.4 %copy-start.18 = (bf16[256,256]{1,0:T(8,128)(2,1)S(1)}, bf16[256,256]{1,0:T(8,128)(2,1)}, u32[]{:S(2)}) copy-start(bf16[256,256]{1,0:T(8,128)(2,1)} %constant.46.clone.band_high) | copy-start | bytes 393220
  85.7 0.9 copy-start.20
  86.6 2.5 %copy-start.22 = (f32[2560,512]{1,0:T(8,128)S(1)}, f32[2560,512]{1,0:T(8,128)}, u32[]{:S(2)}) copy-start(f32[2560,512]{1,0:T(8,128)} %copy-done.21) | copy-start | bytes 15728644
  95.6 11.0 %all-to-all-start.2 = ((bf16[8,80,128]{2,1,0:T(8,128)(2,1)}), bf16[8,80,128]{2,1,0:T(8,128)(2,1)S(1)}, u32[]{:S(2)}, u32[]{:S(2)}) async-start(bf16[8,80,128]{2,1,0:T(8,128)(2,1)} %broadcast_in_dim.13), calls=%async_computation.2 | async-start | bytes 327680 | tf_op jit(solution)/shard_map/all_to_all | solution.py:210
  107.3 1.1 copy-start.1
  108.4 1.0 copy-start.2
  109.3 0.9 copy-start.3
  110.2 0.9 copy-start.13
  111.1 0.9 copy-start.15
  122.7 22.5 %all-to-all-start.4 = ((bf16[32,40,128]{2,1,0:T(8,128)(2,1)}), bf16[32,40,128]{2,1,0:T(8,128)(2,1)S(1)}, u32[]{:S(2)}, u32[]{:S(2)}) async-start(bf16[32,40,128]{2,1,0:T(8,128)(2,1)} %reshape.38), calls=%async_computation.4 | async-start | bytes 655360 | tf_op jit(solution)/shard_map/all_to_all | solution.py:238
  127.7 0.8 copy-start.4
  128.5 0.8 copy-start.6
  129.3 1.6 %copy-start.8 = (bf16[1,448,2560]{2,1,0:T(8,128)(2,1)S(1)}, bf16[1,448,2560]{2,1,0:T(8,128)(2,1)}, u32[]{:S(2)}) copy-start(bf16[1,448,2560]{2,1,0:T(8,128)(2,1)} %momentum.3) | copy-start | bytes 6881284
  130.9 1.0 copy-start.9
  132.0 1.0 copy-start.10
  133.0 0.9 copy-start.14
  133.9 0.9 copy-start.16

commit v2 on v0

v2 whole, which is shorter than its diff:
```python
import jax
import jax.numpy as jnp
import ml_dtypes
import numpy as np
from jax import lax
from jax.experimental import pallas as pl
from jax.experimental.pallas import tpu as pltpu
from jax.sharding import PartitionSpec as P

TILE = 64
BETA_DECAY = 0.9
STEP_RATE = 0.1
PACK = 16
SPAN = 512
BAND = 256
HALF = 256
RING = 4
F32 = jnp.float32
BF16 = jnp.bfloat16


def cosine_table():
    freq = np.arange(TILE, dtype=np.float64)[:, None]
    place = np.arange(TILE, dtype=np.float64)[None, :]
    table = np.cos(np.pi * (2.0 * place + 1.0) * freq / (2.0 * TILE))
    return table * np.where(freq == 0.0, np.sqrt(1.0 / TILE), np.sqrt(2.0 / TILE))


def parts(table):
    high = table.astype(np.float32).astype(ml_dtypes.bfloat16)
    low = (table - high.astype(np.float64)).astype(np.float32).astype(ml_dtypes.bfloat16)
    return high, low


def row_table(rows):
    cosine = cosine_table()
    table = np.zeros((2 * HALF, 2 * HALF))
    for i in range(rows // TILE):
        for p in range(2):
            lanes = slice(p * HALF + i * (TILE // 2), p * HALF + (i + 1) * (TILE // 2))
            table[i * TILE : (i + 1) * TILE, lanes] = cosine[p::2].T
    return table


def band_table():
    return np.kron(np.eye(BAND // TILE), cosine_table())


def split(value):
    high = value.astype(BF16)
    return high, (value - high.astype(F32)).astype(BF16)


def dot(a, b):
    return jnp.dot(a, b, preferred_element_type=F32)


def dot_turned(a, b):
    return lax.dot_general(a, b, (((1,), (1,)), ((), ())), preferred_element_type=F32)


def momentum_spectrum_kernel(momentum, row_pair, band, out, held, twice, stack, ready, incoming, outgoing):
    steps, rows, span = held.shape

    def load(step):
        return pltpu.make_async_copy(momentum.at[0, :, pl.ds(step * span, span)], held.at[step], incoming.at[step])

    def store(step):
        return pltpu.make_async_copy(ready.at[step], out.at[pl.ds(step * span, span), :], outgoing.at[step])

    for step in range(steps):
        load(step).start()
    twice[...] = jnp.zeros_like(twice)
    bands = jnp.concatenate([band[...], band[:, :BAND]], axis=1)
    for step in range(steps):
        load(step).wait()
        turned = held[step].T
        twice[:, :rows] = turned
        twice[:, 2 * HALF : 2 * HALF + rows] = turned
        high, low = split(BETA_DECAY * dot(twice[...], row_pair[...]))
        for start in range(0, span, BAND):
            stack[:BAND] = high[start : start + BAND]
            stack[BAND : 2 * BAND] = high[start : start + BAND]
            stack[2 * BAND :] = low[start : start + BAND]
            ready[step, start : start + BAND] = dot(bands, stack[...])
        store(step).start()
    for step in range(steps):
        store(step).wait()


def weight_loads(place, gate, up, gate_held, up_held, arrived):
    width = gate.shape[1] // RING
    loads = []
    for step in range(RING):
        owner = lax.rem(place[0] + RING - step, RING)
        columns = pl.ds(pl.multiple_of(owner * width, 128), width)
        loads.append(pltpu.make_async_copy(gate.at[:, columns], gate_held.at[step], arrived.at[2 * step]))
        loads.append(pltpu.make_async_copy(up.at[:, columns], up_held.at[step], arrived.at[2 * step + 1]))
    return loads


def ring_swiglu(loads, features, gate_held, up_held):
    gated = upper = None
    for step, feature in enumerate(features):
        loads[2 * step].wait()
        term = dot(gate_held[step], feature)
        gated = term if gated is None else gated + term
        loads[2 * step + 1].wait()
        term = dot(up_held[step], feature)
        upper = term if upper is None else upper + term
    return (gated / (1.0 + jnp.exp(-gated)) * upper).astype(BF16)


def pick_kernel(place, *refs):
    pieces = refs[:RING]
    gate, up, row_pair, band, spectrum, offsets, whole_grads, hidden, own, sent = refs[RING : RING + 10]
    gate_held, up_held, spectra, grads, factor, arrived, spectra_arrived = refs[RING + 10 :]
    rows, count = hidden.shape
    width = whole_grads.shape[0] // RING
    depth = pieces[0].shape[0]
    features = width // depth
    loads = weight_loads(place, gate, up, gate_held, up_held, arrived)
    owners = [lax.rem(place[0] + RING - step, RING) for step in range(RING)]
    spectrum_loads = [
        pltpu.make_async_copy(
            spectrum.at[pl.ds(pl.multiple_of(owners[step] * width, 128), width), :],
            spectra.at[step],
            spectra_arrived.at[step],
        )
        for step in range(RING)
    ]
    for load in loads + spectrum_loads:
        load.start()
    turned = ring_swiglu(
        loads, [piece[:, :features].reshape(width, count) for piece in pieces], gate_held, up_held
    )
    hidden[...] = turned
    turned = turned.T
    high, low = split(dot(turned, row_pair[:rows]) + dot(turned, row_pair[2 * HALF : 2 * HALF + rows]))
    factor[:count] = high
    factor[count : 2 * count] = high
    factor[2 * count :] = low

    column = lax.broadcasted_iota(jnp.int32, (TILE, HALF), 0)
    for step, piece in enumerate(pieces):
        block = piece[:, features:].reshape(width, count)
        whole_grads[pl.ds(pl.multiple_of(owners[step] * width, 128), width), :] = block
        for start in range(0, width, BAND):
            size = min(BAND, width - start)
            part = block[start : start + size]
            high, low = split(dot(band[:size, :size], part) + dot(band[:size, BAND : BAND + size], part))
            grads[start : start + size, :count] = high
            grads[start : start + size, count : 2 * count] = low
            grads[start : start + size, 2 * count :] = high
        spectrum_loads[step].wait()
        total = spectra.at[step]
        total[...] += dot(grads[...], factor[...])
        for k in range(width // TILE):
            tile = owners[step] * (width // TILE) + k
            spots = offsets[place[1], pl.ds(tile, 1), :]
            even = total[k * TILE : (k + 1) * TILE, :HALF]
            odd = total[k * TILE : (k + 1) * TILE, HALF:]
            hit = jnp.where(spots == column, even, jnp.where(spots == column + TILE, odd, 0.0))
            own[pl.ds(tile, 1), :] = jnp.sum(hit, axis=0, keepdims=True)
    value = own[...].astype(BF16).astype(F32)
    own[...] = value
    packed = jnp.concatenate([value[:, : HALF // 2], value[:, HALF // 2 :]], axis=0).astype(BF16)
    for r in range(sent.shape[0]):
        sent[r] = packed


def next_kernel(place, *refs):
    pieces = refs[:RING]
    gate, up, down, row_pair, base, factor = refs[RING : RING + 6]
    gate_held, up_held, down_held, arrived, down_arrived = refs[RING + 6 :]
    count = base.shape[0]
    rows = down.shape[0]
    loads = weight_loads(place, gate, up, gate_held, up_held, arrived)
    down_load = pltpu.make_async_copy(down, down_held, down_arrived.at[0])
    for load in loads:
        load.start()
    down_load.start()
    features = []
    for piece in pieces:
        value = piece[...].astype(F32)
        blocks = []
        for d in range(value.shape[0]):
            blocks += [value[d, :, :count], value[d, :, count:]]
        features.append(jnp.concatenate(blocks, axis=0).astype(BF16))
    turned = ring_swiglu(loads, features, gate_held, up_held).T
    along = (dot(turned, row_pair[:rows]) + dot(turned, row_pair[2 * HALF : 2 * HALF + rows])).T
    factor[...] = jnp.concatenate(split(along), axis=1)
    down_load.wait()
    base[...] = dot(turned, down_held[...])


def output_kernel(values, offsets, next_rows, base, back, out, dense, across, rearranged, columns, even_values, odd_values):
    replicas, tile_cols, _ = offsets.shape
    tokens = base.shape[0]
    bands = base.shape[1] // BAND
    chunks = base.shape[1] // 128
    for r in range(replicas):
        value = values[r].astype(F32)
        value = jnp.concatenate([value[:tile_cols], value[tile_cols:]], axis=1)
        columns[r] = (offsets[r] & (TILE - 1)).astype(F32)
        even_values[r] = jnp.where(offsets[r] < TILE, value, 0.0)
        odd_values[r] = jnp.where(offsets[r] < TILE, 0.0, value)
    place = lax.broadcasted_iota(jnp.int32, (TILE, 128), 0).astype(F32).astype(BF16)
    zero = jnp.zeros((PACK, 128), BF16)

    def one(tile, carry):
        for start in range(0, HALF, 128):
            listed = []
            for r in range(replicas):
                rows = (table[r, pl.ds(tile, 1), :][:, start : start + 128] for table in (columns, even_values, odd_values))
                listed.append([jnp.broadcast_to(row, (PACK, 128)).astype(BF16) for row in rows])
            for first in range(0, TILE, PACK):
                even, odd = zero, zero
                for spots, even_value, odd_value in listed:
                    hit = spots == place[first : first + PACK]
                    even += jnp.where(hit, even_value, zero)
                    odd += jnp.where(hit, odd_value, zero)
                row = pl.ds(pl.multiple_of(tile * TILE + first, PACK), PACK)
                dense[row, start : start + 128] = even
                dense[row, HALF + start : HALF + start + 128] = odd
        return carry

    lax.fori_loop(0, tile_cols, one, 0)
    for step in range(0, bands, 2):
        both = dot(dense[step * BAND : (step + 2) * BAND], next_rows[...]).astype(BF16)
        for k in range(2):
            part = both[k * BAND : (k + 1) * BAND]
            across[:BAND, (step + k) * 128 : (step + k + 1) * 128] = part
            across[BAND:, (step + k) * 128 : (step + k + 1) * 128] = part
    change = dot(back[...], across[...])
    for step in range(bands):
        turned = change[:, step * 128 : (step + 1) * 128].T
        result = base[:, step * BAND : (step + 1) * BAND] - (STEP_RATE / replicas) * (turned[:tokens] + turned[tokens:])
        for c in range(BAND // 128):
            rearranged[pl.ds(step * (BAND // 128) + c, tokens, stride=chunks), :] = result[:, c * 128 : (c + 1) * 128]
    out[...] = rearranged[...].astype(BF16)


def kept_kernel(
    place, own, offsets, cotangent, hidden, momentum, row_pair, back, out, held, ready, dense, left, right, incoming, outgoing
):
    steps, rows, span = held.shape
    spectral = 2 * HALF

    def load(step):
        return pltpu.make_async_copy(momentum.at[0, :, pl.ds(step * span, span)], held.at[step], incoming.at[step])

    def store(step):
        return pltpu.make_async_copy(ready.at[step], out.at[0, :, pl.ds(step * span, span)], outgoing.at[step])

    for step in range(steps):
        load(step).start()
    left[:, :spectral] = row_pair[:rows]
    left[:, spectral : 2 * spectral] = row_pair[:rows]
    left[:, 2 * spectral : 3 * spectral] = row_pair[spectral : spectral + rows]
    left[:, 3 * spectral :] = -hidden[...]
    column = lax.broadcasted_iota(jnp.int32, (TILE, HALF), 0)
    for step in range(steps):
        for start in range(0, span, BAND):
            for k in range(BAND // TILE):
                tile = (step * span + start) // TILE + k
                spots, value = offsets[place[1], tile : tile + 1, :], own[tile : tile + 1, :]
                even = jnp.where(spots == column, value, 0.0).astype(BF16)
                odd = jnp.where(spots == column + TILE, value, 0.0).astype(BF16)
                for copy in range(2):
                    dense[copy * BAND + k * TILE : copy * BAND + (k + 1) * TILE, :HALF] = even
                    dense[copy * BAND + k * TILE : copy * BAND + (k + 1) * TILE, HALF:] = odd
            high, low = split(dot(back[...], dense[...]))
            right[start : start + BAND, :spectral] = high
            right[start : start + BAND, spectral : 2 * spectral] = low
            right[start : start + BAND, 2 * spectral : 3 * spectral] = high
        right[:, 3 * spectral :] = cotangent[step * span : (step + 1) * span]
        change = dot_turned(left[...], right[...])
        load(step).wait()
        ready[step] = (BETA_DECAY * held[step].astype(F32) - change).astype(BF16)
        store(step).start()
    for step in range(steps):
        store(step).wait()


IN_VMEM = pl.BlockSpec(memory_space=pltpu.VMEM)
IN_SMEM = pl.BlockSpec(memory_space=pltpu.SMEM)
IN_HBM = pl.BlockSpec(memory_space=pltpu.HBM)


def params(limit=58):
    return pltpu.CompilerParams(vmem_limit_bytes=limit * 1024 * 1024)


def cost(flops, moved):
    return pl.CostEstimate(flops=int(flops), bytes_accessed=int(moved), transcendentals=0)


def depth_gather(block, depth):
    groups = [[x * depth + z for z in range(depth)] for x in range(RING)]
    blocks = jnp.broadcast_to(block[None], (depth,) + block.shape)
    return lax.all_to_all(blocks, "tensor", 0, 0, tiled=True, axis_index_groups=groups)


def ring_gather(block, depth):
    pieces = [block]
    for step in range(1, RING):
        pairs = [(x * depth + z, (x + step) % RING * depth + z) for x in range(RING) for z in range(depth)]
        pieces.append(lax.ppermute(block, "tensor", pairs))
    return pieces


def on_device(tokens, next_tokens, cotangent, gate_weight, up_weight, down_weight, momentum, indices):
    shards = lax.axis_size("tensor")
    depth = shards // RING
    replicas = lax.axis_size("replica")
    place = jnp.stack([lax.axis_index("tensor") // depth, lax.axis_index("replica")]).astype(jnp.int32)
    rows, width = down_weight.shape
    bands = width // BAND
    part = width // RING
    tile_rows, tile_cols, keep = indices.shape[1:]
    stride = TILE * TILE // keep
    count, next_count, features = tokens.shape[0], next_tokens.shape[0], tokens.shape[1]
    row_pair = jnp.asarray(np.concatenate(parts(row_table(rows))))
    band = jnp.asarray(np.concatenate(parts(band_table()), axis=1))
    back = jnp.asarray(np.concatenate(parts(band_table().T), axis=1))
    gate, up = gate_weight.T, up_weight.T

    turned = next_tokens.T
    packed = jnp.concatenate([turned[: features // 2], turned[features // 2 :]], axis=1)
    gathered = depth_gather(jnp.concatenate([tokens.T, cotangent.T, packed]), depth)
    pieces = ring_gather(gathered[:, : 2 * features], depth)
    nexts = ring_gather(gathered[:, 2 * features :], depth)

    offsets = indices - jnp.arange(keep, dtype=jnp.int32) * stride
    offsets = offsets.transpose(0, 2, 1, 3).reshape(replicas, tile_cols, tile_rows * keep)
    offsets = jnp.pad(offsets, ((0, 0), (0, 0), (0, HALF - tile_rows * keep)), constant_values=-1)

    def shape(dims, kind):
        return jax.ShapeDtypeStruct(dims, kind)

    dma = pltpu.SemaphoreType.DMA
    weights_held = [pltpu.VMEM((RING, rows, part), BF16)] * 2

    spectrum = pl.pallas_call(
        momentum_spectrum_kernel,
        in_specs=[IN_HBM, IN_VMEM, IN_VMEM],
        out_specs=IN_HBM,
        out_shape=shape((width, 2 * HALF), F32),
        scratch_shapes=[
            pltpu.VMEM((width // SPAN, rows, SPAN), BF16),
            pltpu.VMEM((SPAN, 4 * HALF), BF16),
            pltpu.VMEM((3 * BAND, 2 * HALF), BF16),
            pltpu.VMEM((width // SPAN, SPAN, 2 * HALF), F32),
            dma((width // SPAN,)),
            dma((width // SPAN,)),
        ],
        compiler_params=params(),
        cost_estimate=cost(6e9, 8e6),
        name="momentum_spectrum",
    )(momentum, row_pair, band)

    whole_grads, hidden, own, sent = pl.pallas_call(
        pick_kernel,
        in_specs=[IN_SMEM] + [IN_VMEM] * RING + [IN_HBM] * 2 + [IN_VMEM] * 2 + [IN_HBM, IN_VMEM],
        out_specs=[IN_VMEM] * 4,
        out_shape=[
            shape((width, count), BF16),
            shape((rows, count), BF16),
            shape((tile_cols, HALF), F32),
            shape((replicas, 2 * tile_cols, HALF // 2), BF16),
        ],
        scratch_shapes=weights_held
        + [
            pltpu.VMEM((RING, part, 2 * HALF), F32),
            pltpu.VMEM((part, 3 * count), BF16),
            pltpu.VMEM((3 * count, 2 * HALF), BF16),
            dma((2 * RING,)),
            dma((RING,)),
        ],
        compiler_params=params(),
        cost_estimate=cost(6e9, 12e6),
        name="pick",
    )(place, *pieces, gate, up, row_pair, band, spectrum, offsets)

    listed = lax.all_to_all(sent, "replica", 0, 0, tiled=True)

    base, next_rows = pl.pallas_call(
        next_kernel,
        in_specs=[IN_SMEM] + [IN_VMEM] * RING + [IN_HBM] * 3 + [IN_VMEM],
        out_specs=[IN_VMEM] * 2,
        out_shape=[shape((next_count, width), F32), shape((2 * HALF, 2 * next_count), BF16)],
        scratch_shapes=weights_held + [pltpu.VMEM((rows, width), BF16), dma((2 * RING,)), dma((1,))],
        compiler_params=params(),
        cost_estimate=cost(2e9, 7e6),
        name="next_hidden",
    )(place, *nexts, gate, up, down_weight, row_pair)

    partial = pl.pallas_call(
        output_kernel,
        in_specs=[IN_VMEM] * 5,
        out_specs=IN_VMEM,
        out_shape=shape((next_count * width // 128, 128), BF16),
        scratch_shapes=[
            pltpu.VMEM((width, 2 * HALF), BF16),
            pltpu.VMEM((2 * BAND, bands * 2 * next_count), BF16),
            pltpu.VMEM((next_count * width // 128, 128), F32),
        ]
        + [pltpu.VMEM((replicas, tile_cols, HALF), F32)] * 3,
        compiler_params=params(),
        cost_estimate=cost(4e9, 4e6),
        name="output_part",
    )(listed, offsets, next_rows, base, back)

    received = lax.all_to_all(partial.reshape(shards, -1, 128), "tensor", 0, 0, tiled=True)
    output = jnp.sum(received.astype(F32), axis=0).astype(BF16).reshape(next_count // shards, width)

    kept = pl.pallas_call(
        kept_kernel,
        in_specs=[IN_SMEM] + [IN_VMEM] * 4 + [IN_HBM, IN_VMEM, IN_VMEM],
        out_specs=IN_HBM,
        out_shape=shape((1, rows, width), BF16),
        scratch_shapes=[pltpu.VMEM((width // SPAN, rows, SPAN), BF16)] * 2
        + [
            pltpu.VMEM((2 * BAND, 2 * HALF), BF16),
            pltpu.VMEM((rows, 6 * HALF + count), BF16),
            pltpu.VMEM((SPAN, 6 * HALF + count), BF16),
            dma((width // SPAN,)),
            dma((width // SPAN,)),
        ],
        compiler_params=params(),
        cost_estimate=cost(10e9, 8e6),
        name="kept",
    )(place, own, offsets, whole_grads, hidden, momentum, row_pair, back)
    return (output, kept)


def solution(mesh):
    return jax.shard_map(
        on_device,
        mesh=mesh,
        in_specs=(
            P("replica", "tensor"),
            P("replica", "tensor"),
            P("replica", "tensor"),
            P(None, "tensor"),
            P(None, "tensor"),
            P("tensor", None),
            P("replica", "tensor", None),
            P(None, "tensor", None, None),
        ),
        out_specs=(P(("replica", "tensor"), None), P("replica", "tensor", None)),
        check_vma=False,
    )
```

time: 664 us -> 96.6 us (0.15)
  local copies, waits for them, and re-layouts: 213 us -> 5.97 us
  blocking collectives: 166 us -> 0 us
  matrix products: 106 us -> 0 us
  other arithmetic: 75.9 us -> 1.71 us
  waiting for transfers between devices: 79.4 us -> 15.6 us
  Pallas kernels: 0 us -> 43.1 us
  starting transfers between devices: 0.04 us -> 28.7 us
  between operations: 15.1 us -> 0.8 us
    all_gather x4 -> x0, blocking collectives: 166 us -> none  [the longest x1 52.1 us: on_device(): lax.all_gather(cotangent, 'tensor', axis=1, tiled=True)]
    dot_general x10 -> x0, matrix products: 106 us -> none  [the longest x4 61.6 us: inverse_tiles(): jnp.einsum('ak,xyab,bl->xkyl', table, blocks, table, precision=lax.Precis...]
    mul x20 -> x0, local copies, waits for them, and re-layouts: 86.2 us -> none  [the longest x18 69.1 us: place_values(): placed = values[..., None] * one_hot_slots(where)]
    eq x28 -> x0, local copies, waits for them, and re-layouts: 81.6 us -> none  [one_hot_slots(): return (offset[..., None] == slots).astype(jnp.float32)]
    unnamed x2 -> x0, waiting for transfers between devices: 79.4 us -> none
    add x8 -> x0, other arithmetic: 68.6 us -> none  [add_replica(): return dense + place_values(values, spots)]
    pallas_call x0 -> x5, Pallas kernels: none -> 43.1 us  [the longest x1 10.3 us: on_device(): pl.pallas_call(kept_kernel, in_specs=[IN_SMEM] + [IN_VMEM] * 4 + [IN_HBM,...]
    reshape x3 -> x2, local copies, waits for them, and re-layouts: 24.5 us -> 0.92 us  [the longest x1 0.61 us: on_device(): jnp.sum(received.astype(F32), axis=0).astype(BF16)]
  transfers between devices with their start and end apart: 1 -> 9, of which waited for: 1 -> 4; matrix products, arithmetic and copies ran while one was open for 9% -> 2% of each run, Pallas kernels for 0% -> 39%
where the time goes in v2:
time: 96.6 us; the launch traced here: 95.8 us
  Pallas kernels  43.1 us (45%)
  starting transfers between devices  28.7 us (30%)
  waiting for transfers between devices  15.6 us (16%)
  local copies, waits for them, and re-layouts  5.97 us (6%)
  other arithmetic  1.71 us (2%)
    pallas_call x1, Pallas kernels, on_device(): pl.pallas_call(kept_kernel, in_specs=[IN_SMEM] + [IN_VMEM] * 4 + [IN_HBM,...  10.3 us
    pallas_call x1, Pallas kernels, on_device(): pl.pallas_call(pick_kernel, in_specs=[IN_SMEM] + [IN_VMEM] * RING + [IN_H...  9.8 us
    pallas_call x1, Pallas kernels, on_device(): pl.pallas_call(momentum_spectrum_kernel, in_specs=[IN_HBM, IN_VMEM, IN_VM...  9.6 us
    all_to_all x1, starting transfers between devices, depth_gather(): lax.all_to_all(blocks, 'tensor', 0, 0, tiled=True, axis_index_groups=groups)  8.57 us
    ppermute x6, starting transfers between devices, ring_gather(): pieces.append(lax.ppermute(block, 'tensor', pairs))  8.03 us
    all_to_all x1, starting transfers between devices, on_device(): lax.all_to_all(partial.reshape(shards, -1, 128), 'tensor', 0, 0, tiled=True)  7.58 us
    ppermute x6, waiting for transfers between devices, ring_gather(): pieces.append(lax.ppermute(block, 'tensor', pairs))  7.42 us
    pallas_call x1, Pallas kernels, on_device(): pl.pallas_call(next_kernel, in_specs=[IN_SMEM] + [IN_VMEM] * RING + [IN_H...  7.23 us
  transfers between devices with their start and end apart: 9, of which 4 were waited for; matrix products, arithmetic and copies ran while one was open for 2% of the time, Pallas kernels for 39%

profile of v2, /device:TPU:32, one launch (start us, length us, event | category | flops | bytes accessed | tf_op | source)
XLA Modules:
  0.0 95.8 jit_solution(8736772285564612013)
XLA Ops:
  0.6 0.8 copy.15
  1.4 0.8 maximum_maximum_fusion
  2.3 0.8 broadcast_in_dim.2
  3.1 8.6 %all-to-all-start = ((bf16[8,200,128]{2,1,0:T(8,128)(2,1)}), bf16[8,200,128]{2,1,0:T(8,128)(2,1)S(1)}, u32[]{:S(2)}, u32[]{:S(2)}) async-start(bf16[8,200,128]{2,1,0:T(8,128)(2,1)} %broadcast_in_dim.2), calls=%async_computation | async-start | bytes 819200 | tf_op jit(solution)/shard_map/all_to_all | solution.py:302
  11.7 0.0 copy-start
  11.7 9.6 %momentum_spectrum.1.refs_8_ = f32[2560,512]{1,0:T(8,128)} custom-call(bf16[1,448,2560]{2,1,0:T(8,128)(2,1)} %momentum.3, bf16[1024,512]{1,0:T(8,128)(2,1)} %constant.37.clone.row_pair.refs_6_.refs_7_, bf16[256,512]{1,0:T(8,128)(2,1)} %constant.38.clone.band.refs_7_), custom_call_target="tpu_custom_call" | custom-call | flops 6000000000 | bytes 8000000 | tf_op jit(solution)/shard_map/momentum_spectrum/pallas_call | solution.py:345
  21.3 4.0 %all-to-all-done = bf16[8,200,128]{2,1,0:T(8,128)(2,1)S(1)} async-done(((bf16[8,200,128]{2,1,0:T(8,128)(2,1)}), bf16[8,200,128]{2,1,0:T(8,128)(2,1)S(1)}, u32[]{:S(2)}, u32[]{:S(2)}) %all-to-all-start) | async-done | bytes 409632 | tf_op jit(solution)/shard_map/all_to_all | solution.py:302
  25.3 0.0 copy-start.2
  25.3 1.6 %collective-permute-start = (bf16[8,160,128]{2,1,0:T(8,128)(2,1)S(1)}, bf16[8,160,128]{2,1,0:T(8,128)(2,1)S(1)}, u32[]{:S(2)}, u32[]{:S(2)}) collective-permute-start(bf16[8,160,128]{2,1,0:T(8,128)(2,1)S(1)} %slice.18.refs_0_), channel_id=1, source_target_pairs={{0,8},{1,9},{2,10},{3,11},{4,12},{5,13},{6,14},{7,15},{8,16},{9,17... | collective-permute-start | bytes 983048 | tf_op jit(solution)/shard_map/ppermute | solution.py:309
  26.8 2.7 %collective-permute-start.1 = (bf16[8,160,128]{2,1,0:T(8,128)(2,1)S(1)}, bf16[8,160,128]{2,1,0:T(8,128)(2,1)S(1)}, u32[]{:S(2)}, u32[]{:S(2)}) collective-permute-start(bf16[8,160,128]{2,1,0:T(8,128)(2,1)S(1)} %slice.18.refs_0_), channel_id=1, source_target_pairs={{0,16},{1,17},{2,18},{3,19},{4,20},{5,21},{6,22},{7,23},{8,24},{9,... | collective-permute-start | bytes 983048 | tf_op jit(solution)/shard_map/ppermute | solution.py:309
  29.6 1.4 %collective-permute-start.2 = (bf16[8,160,128]{2,1,0:T(8,128)(2,1)S(1)}, bf16[8,160,128]{2,1,0:T(8,128)(2,1)}, u32[]{:S(2)}, u32[]{:S(2)}) collective-permute-start(bf16[8,160,128]{2,1,0:T(8,128)(2,1)S(1)} %slice.18.refs_0_), channel_id=1, source_target_pairs={{0,24},{1,25},{2,26},{3,27},{4,28},{5,29},{6,30},{7,31},{8,0},{9,1... | collective-permute-start | bytes 983048 | tf_op jit(solution)/shard_map/ppermute | solution.py:309
  31.0 0.0 copy-done
  31.0 0.2 broadcast_subtract_fusion
  31.2 0.3 copy.17
  31.5 0.8 pad.4.refs_9_.offsets
  32.3 0.6 pad_add_fusion.place
  32.9 0.0 copy-start.1
  32.9 0.7 collective-permute-start.3
  33.6 0.9 collective-permute-start.4
  34.5 3.5 %collective-permute-done.refs_1_ = bf16[8,160,128]{2,1,0:T(8,128)(2,1)S(1)} collective-permute-done((bf16[8,160,128]{2,1,0:T(8,128)(2,1)S(1)}, bf16[8,160,128]{2,1,0:T(8,128)(2,1)S(1)}, u32[]{:S(2)}, u32[]{:S(2)}) %collective-permute-start) | collective-permute-done | bytes 327712 | tf_op jit(solution)/shard_map/ppermute | solution.py:309
  38.0 0.0 copy-start.7
  38.0 0.8 collective-permute-start.5
  38.8 3.9 %collective-permute-done.1.refs_2_ = bf16[8,160,128]{2,1,0:T(8,128)(2,1)S(1)} collective-permute-done((bf16[8,160,128]{2,1,0:T(8,128)(2,1)S(1)}, bf16[8,160,128]{2,1,0:T(8,128)(2,1)S(1)}, u32[]{:S(2)}, u32[]{:S(2)}) %collective-permute-start.1) | collective-permute-done | bytes 327712 | tf_op jit(solution)/shard_map/ppermute | solution.py:309
  42.6 0.0 collective-permute-done.2.refs_3_
  42.6 0.0 copy-done.2
  42.7 0.0 copy-done.7
  42.7 0.7 copy-done.8
  43.4 9.8 %pick.1 = (bf16[2560,128]{1,0:T(8,128)(2,1)}, bf16[448,128]{1,0:T(8,128)(2,1)}, f32[40,256]{1,0:T(8,128)}, bf16[8,80,128]{2,1,0:T(8,128)(2,1)}) custom-call(s32[2]{0:T(128)} %pad_add_fusion.place, bf16[8,160,128]{2,1,0:T(8,128)(2,1)} %copy-done.2, bf16[8,160,128]{2,1,0:T(8,128)(2,1)} %copy-done.7, bf16[8,160,128]{2,1,0:T(8,128)(2,1)} %copy-done.8, ...), custom_call_target="tpu_custom_call" | custom-call | flops 6000000000 | bytes 12000000 | tf_op jit(solution)/shard_map/pick/pallas_call | solution.py:363
  53.2 0.0 copy-done.1
  53.2 4.5 %all-to-all-start.1 = ((bf16[8,80,128]{2,1,0:T(8,128)(2,1)}), bf16[8,80,128]{2,1,0:T(8,128)(2,1)S(1)}, u32[]{:S(2)}, u32[]{:S(2)}) async-start(bf16[8,80,128]{2,1,0:T(8,128)(2,1)} %get-tuple-element.8), calls=%async_computation.1 | async-start | bytes 327680 | tf_op jit(solution)/shard_map/all_to_all | solution.py:386
  57.7 0.0 collective-permute-done.3.refs_1_
  57.7 0.0 copy-start.4
  57.7 0.0 collective-permute-done.4.refs_2_
  57.7 0.0 copy-start.5
  57.7 0.0 collective-permute-done.5.refs_3_
  57.7 0.6 copy-done.4
  58.3 0.0 copy-done.5
  58.3 0.6 copy-done.6
  59.0 7.2 %next_hidden.1 = (f32[64,2560]{1,0:T(8,128)}, bf16[512,128]{1,0:T(8,128)(2,1)}) custom-call(s32[2]{0:T(128)} %pad_add_fusion.place, bf16[8,40,128]{2,1,0:T(8,128)(2,1)} %copy-done.1, bf16[8,40,128]{2,1,0:T(8,128)(2,1)} %copy-done.4, bf16[8,40,128]{2,1,0:T(8,128)(2,1)} %copy-done.5, bf16[8,40,128]{2,1,0:T(8,128)(2,1)} %copy-done.6, ...), custom_call_target="tpu_custom_call" | custom-call | flops 2000000000 | bytes 7000000 | tf_op jit(solution)/shard_map/next_hidden/pallas_call | solution.py:388
  66.2 0.0 all-to-all-done.1.values
  66.2 0.0 copy-start.3
  66.2 0.6 copy-done.3
  66.9 6.1 %output_part.1 = bf16[1280,128]{1,0:T(8,128)(2,1)} custom-call(bf16[8,80,128]{2,1,0:T(8,128)(2,1)} %copy-done.3, s32[8,40,256]{2,1,0:T(8,128)} %pad.4.refs_9_.offsets, bf16[512,128]{1,0:T(8,128)(2,1)} %get-tuple-element.9.next_rows, f32[64,2560]{1,0:T(8,128)} %get-tuple-element.10.base, bf16[256,512]{1,0:T(8,128)(2,1)} %constant.39.clone.back), custom_call_target="tpu_custom_call" | custom-call | flops 4000000000 | bytes 4000000 | tf_op jit(solution)/shard_map/output_part/pallas_call | solution.py:399
  73.0 7.6 %all-to-all-start.2 = ((bf16[32,40,128]{2,1,0:T(8,128)(2,1)}), bf16[32,40,128]{2,1,0:T(8,128)(2,1)S(1)}, u32[]{:S(2)}, u32[]{:S(2)}) async-start(bf16[32,40,128]{2,1,0:T(8,128)(2,1)} %bitcast.16), calls=%async_computation.2 | async-start | bytes 655360 | tf_op jit(solution)/shard_map/all_to_all | solution.py:415
  80.6 10.3 %kept.1 = bf16[1,448,2560]{2,1,0:T(8,128)(2,1)} custom-call(s32[2]{0:T(128)} %pad_add_fusion.place, f32[40,256]{1,0:T(8,128)} %get-tuple-element.11.own, s32[8,40,256]{2,1,0:T(8,128)} %pad.4.refs_9_.offsets, bf16[2560,128]{1,0:T(8,128)(2,1)} %get-tuple-element.12.cotangent, bf16[448,128]{1,0:T(8,128)(2,1)} %get-tuple-element.13.hidden, ...), custom_call_target="tpu_custom_call" | custom-call | flops 10000000000 | bytes 8000000 | tf_op jit(solution)/shard_map/kept/pallas_call | solution.py:418
  90.9 4.2 %all-to-all-done.2 = bf16[32,40,128]{2,1,0:T(8,128)(2,1)S(1)} async-done(((bf16[32,40,128]{2,1,0:T(8,128)(2,1)}), bf16[32,40,128]{2,1,0:T(8,128)(2,1)S(1)}, u32[]{:S(2)}, u32[]{:S(2)}) %all-to-all-start.2) | async-done | bytes 327712 | tf_op jit(solution)/shard_map/all_to_all | solution.py:415
  95.2 0.1 reduce_sum.12
  95.2 0.6 reshape.20
  (6 shorter events, 0.0 us)
Async XLA Ops:
  3.1 22.1 %all-to-all-start = ((bf16[8,200,128]{2,1,0:T(8,128)(2,1)}), bf16[8,200,128]{2,1,0:T(8,128)(2,1)S(1)}, u32[]{:S(2)}, u32[]{:S(2)}) async-start(bf16[8,200,128]{2,1,0:T(8,128)(2,1)} %broadcast_in_dim.2), calls=%async_computation | async-start | bytes 819200 | tf_op jit(solution)/shard_map/all_to_all | solution.py:302
  11.7 19.4 %copy-start = (s32[8,7,40,32]{2,3,1,0:T(8,128)S(1)}, s32[8,7,40,32]{2,3,1,0:T(8,128)}, u32[]{:S(2)}) copy-start(s32[8,7,40,32]{2,3,1,0:T(8,128)} %param.18) | copy-start | bytes 860164
  25.3 17.4 %copy-start.2 = (bf16[8,160,128]{2,1,0:T(8,128)(2,1)}, bf16[8,160,128]{2,1,0:T(8,128)(2,1)S(1)}, u32[]{:S(2)}) copy-start(bf16[8,160,128]{2,1,0:T(8,128)(2,1)S(1)} %slice.18.refs_0_) | copy-start | bytes 983044
  25.3 12.8 %collective-permute-start = (bf16[8,160,128]{2,1,0:T(8,128)(2,1)S(1)}, bf16[8,160,128]{2,1,0:T(8,128)(2,1)S(1)}, u32[]{:S(2)}, u32[]{:S(2)}) collective-permute-start(bf16[8,160,128]{2,1,0:T(8,128)(2,1)S(1)} %slice.18.refs_0_), channel_id=1, source_target_pairs={{0,8},{1,9},{2,10},{3,11},{4,12},{5,13},{6,14},{7,15},{8,16},{9,17... | collective-permute-start | bytes 983048 | tf_op jit(solution)/shard_map/ppermute | solution.py:309
  26.8 15.8 %collective-permute-start.1 = (bf16[8,160,128]{2,1,0:T(8,128)(2,1)S(1)}, bf16[8,160,128]{2,1,0:T(8,128)(2,1)S(1)}, u32[]{:S(2)}, u32[]{:S(2)}) collective-permute-start(bf16[8,160,128]{2,1,0:T(8,128)(2,1)S(1)} %slice.18.refs_0_), channel_id=1, source_target_pairs={{0,16},{1,17},{2,18},{3,19},{4,20},{5,21},{6,22},{7,23},{8,24},{9,... | collective-permute-start | bytes 983048 | tf_op jit(solution)/shard_map/ppermute | solution.py:309
  29.6 13.1 %collective-permute-start.2 = (bf16[8,160,128]{2,1,0:T(8,128)(2,1)S(1)}, bf16[8,160,128]{2,1,0:T(8,128)(2,1)}, u32[]{:S(2)}, u32[]{:S(2)}) collective-permute-start(bf16[8,160,128]{2,1,0:T(8,128)(2,1)S(1)} %slice.18.refs_0_), channel_id=1, source_target_pairs={{0,24},{1,25},{2,26},{3,27},{4,28},{5,29},{6,30},{7,31},{8,0},{9,1... | collective-permute-start | bytes 983048 | tf_op jit(solution)/shard_map/ppermute | solution.py:309
  32.9 20.3 %copy-start.1 = (bf16[8,40,128]{2,1,0:T(8,128)(2,1)}, bf16[8,40,128]{2,1,0:T(8,128)(2,1)S(1)}, u32[]{:S(2)}) copy-start(bf16[8,40,128]{2,1,0:T(8,128)(2,1)S(1)} %slice.19.refs_0_) | copy-start | bytes 245764
  32.9 24.7 %collective-permute-start.3 = (bf16[8,40,128]{2,1,0:T(8,128)(2,1)S(1)}, bf16[8,40,128]{2,1,0:T(8,128)(2,1)S(1)}, u32[]{:S(2)}, u32[]{:S(2)}) collective-permute-start(bf16[8,40,128]{2,1,0:T(8,128)(2,1)S(1)} %slice.19.refs_0_), channel_id=1, source_target_pairs={{0,8},{1,9},{2,10},{3,11},{4,12},{5,13},{6,14},{7,15},{8,16},{9,17... | collective-permute-start | bytes 245768 | tf_op jit(solution)/shard_map/ppermute | solution.py:309
  33.6 24.1 %collective-permute-start.4 = (bf16[8,40,128]{2,1,0:T(8,128)(2,1)S(1)}, bf16[8,40,128]{2,1,0:T(8,128)(2,1)S(1)}, u32[]{:S(2)}, u32[]{:S(2)}) collective-permute-start(bf16[8,40,128]{2,1,0:T(8,128)(2,1)S(1)} %slice.19.refs_0_), channel_id=1, source_target_pairs={{0,16},{1,17},{2,18},{3,19},{4,20},{5,21},{6,22},{7,23},{8,24},{9,... | collective-permute-start | bytes 245768 | tf_op jit(solution)/shard_map/ppermute | solution.py:309
  38.0 4.6 %copy-start.7 = (bf16[8,160,128]{2,1,0:T(8,128)(2,1)}, bf16[8,160,128]{2,1,0:T(8,128)(2,1)S(1)}, u32[]{:S(2)}) copy-start(bf16[8,160,128]{2,1,0:T(8,128)(2,1)S(1)} %collective-permute-done.refs_1_) | copy-start | bytes 983044
  38.0 19.7 %collective-permute-start.5 = (bf16[8,40,128]{2,1,0:T(8,128)(2,1)S(1)}, bf16[8,40,128]{2,1,0:T(8,128)(2,1)S(1)}, u32[]{:S(2)}, u32[]{:S(2)}) collective-permute-start(bf16[8,40,128]{2,1,0:T(8,128)(2,1)S(1)} %slice.19.refs_0_), channel_id=1, source_target_pairs={{0,24},{1,25},{2,26},{3,27},{4,28},{5,29},{6,30},{7,31},{8,0},{9,1... | collective-permute-start | bytes 245768 | tf_op jit(solution)/shard_map/ppermute | solution.py:309
  42.6 0.7 copy-start.8
  53.2 13.0 %all-to-all-start.1 = ((bf16[8,80,128]{2,1,0:T(8,128)(2,1)}), bf16[8,80,128]{2,1,0:T(8,128)(2,1)S(1)}, u32[]{:S(2)}, u32[]{:S(2)}) async-start(bf16[8,80,128]{2,1,0:T(8,128)(2,1)} %get-tuple-element.8), calls=%async_computation.1 | async-start | bytes 327680 | tf_op jit(solution)/shard_map/all_to_all | solution.py:386
  57.7 0.6 copy-start.4
  57.7 0.6 copy-start.5
  58.3 0.6 copy-start.6
  66.2 0.7 copy-start.3
  73.0 22.2 %all-to-all-start.2 = ((bf16[32,40,128]{2,1,0:T(8,128)(2,1)}), bf16[32,40,128]{2,1,0:T(8,128)(2,1)S(1)}, u32[]{:S(2)}, u32[]{:S(2)}) async-start(bf16[32,40,128]{2,1,0:T(8,128)(2,1)} %bitcast.16), calls=%async_computation.2 | async-start | bytes 655360 | tf_op jit(solution)/shard_map/all_to_all | solution.py:415

commit v3 on v2

v3 whole, which is shorter than its diff:
```python
import jax
import jax.numpy as jnp
import ml_dtypes
import numpy as np
from jax import lax
from jax.experimental import pallas as pl
from jax.experimental.pallas import tpu as pltpu
from jax.sharding import PartitionSpec as P

TILE = 64
BETA_DECAY = 0.9
STEP_RATE = 0.1
ROOM = 32 << 20
PACK = 16
SPAN = 512
BAND = 256
HALF = 256
RING = 4
F32 = jnp.float32
BF16 = jnp.bfloat16


def cosine_table():
    freq = np.arange(TILE, dtype=np.float64)[:, None]
    place = np.arange(TILE, dtype=np.float64)[None, :]
    table = np.cos(np.pi * (2.0 * place + 1.0) * freq / (2.0 * TILE))
    return table * np.where(freq == 0.0, np.sqrt(1.0 / TILE), np.sqrt(2.0 / TILE))


def parts(table):
    high = table.astype(np.float32).astype(ml_dtypes.bfloat16)
    low = (table - high.astype(np.float64)).astype(np.float32).astype(ml_dtypes.bfloat16)
    return high, low


def row_table(rows):
    cosine = cosine_table()
    table = np.zeros((2 * HALF, 2 * HALF))
    for i in range(rows // TILE):
        for p in range(2):
            lanes = slice(p * HALF + i * (TILE // 2), p * HALF + (i + 1) * (TILE // 2))
            table[i * TILE : (i + 1) * TILE, lanes] = cosine[p::2].T
    return table


def band_table():
    return np.kron(np.eye(BAND // TILE), cosine_table())


def split(value):
    high = value.astype(BF16)
    return high, (value - high.astype(F32)).astype(BF16)


def dot(a, b):
    return jnp.dot(a, b, preferred_element_type=F32)


def dot_turned(a, b):
    return lax.dot_general(a, b, (((1,), (1,)), ((), ())), preferred_element_type=F32)


def pack_kernel(tokens, cotangent, next_tokens, out):
    features, count = tokens.shape
    turned = next_tokens[...].astype(F32).T
    packed = jnp.concatenate([turned[: features // 2], turned[features // 2 :]], axis=1).astype(BF16)
    for d in range(out.shape[0]):
        out[d, :features] = tokens[...]
        out[d, features : 2 * features] = cotangent[...]
        out[d, 2 * features :] = packed


def picked(total, spots):
    column = lax.broadcasted_iota(jnp.int32, (TILE, HALF), 0)
    hit = jnp.where(spots == column, total[:, :HALF], jnp.where(spots == column + TILE, total[:, HALF:], 0.0))
    return jnp.sum(hit, axis=0, keepdims=True)


def momentum_pick_kernel(
    place, momentum, gate, up, row_pair, band, offsets, out, gate_held, up_held, held, twice, stack, incoming, arrived
):
    steps, rows, span = held.shape

    def load(step):
        return pltpu.make_async_copy(momentum.at[0, :, pl.ds(step * span, span)], held.at[step], incoming.at[step])

    for step in range(steps):
        load(step).start()
    weights = weight_loads(place, gate, up, gate_held, up_held, arrived)
    for weight in weights:
        weight.start()
    twice[...] = jnp.zeros_like(twice)
    bands = jnp.concatenate([band[...], band[:, :BAND]], axis=1)
    for step in range(steps):
        load(step).wait()
        turned = held[step].T
        twice[:, :rows] = turned
        twice[:, 2 * HALF : 2 * HALF + rows] = turned
        high, low = split(BETA_DECAY * dot(twice[...], row_pair[...]))
        for start in range(0, span, BAND):
            stack[:BAND] = high[start : start + BAND]
            stack[BAND : 2 * BAND] = high[start : start + BAND]
            stack[2 * BAND :] = low[start : start + BAND]
            total = dot(bands, stack[...])
            for k in range(BAND // TILE):
                tile = (step * span + start) // TILE + k
                spots = offsets[place[1], tile : tile + 1, :]
                out[tile : tile + 1, :] = picked(total[k * TILE : (k + 1) * TILE], spots)
    for weight in weights:
        weight.wait()


def weight_loads(place, gate, up, gate_held, up_held, arrived):
    width = gate.shape[1] // RING
    loads = []
    for step in range(RING):
        owner = lax.rem(place[0] + RING - step, RING)
        columns = pl.ds(pl.multiple_of(owner * width, 128), width)
        loads.append(pltpu.make_async_copy(gate.at[:, columns], gate_held.at[step], arrived.at[2 * step]))
        loads.append(pltpu.make_async_copy(up.at[:, columns], up_held.at[step], arrived.at[2 * step + 1]))
    return loads


def ring_swiglu(features, gate_held, up_held):
    gated = upper = None
    for step, feature in enumerate(features):
        term = dot(gate_held[step], feature)
        gated = term if gated is None else gated + term
        term = dot(up_held[step], feature)
        upper = term if upper is None else upper + term
    return (gated / (1.0 + jnp.exp(-gated)) * upper).astype(BF16)


def pick_kernel(place, *refs):
    pieces = refs[:RING]
    gate_held, up_held, row_pair, band, momentum_part, offsets = refs[RING : RING + 6]
    whole_grads, hidden, next_hidden, sent = refs[RING + 6 : RING + 10]
    grads, total, factor, rows_held, units, next_units, coefficients, packed_held, rows_arrived, left = refs[RING + 10 :]
    rows, count = hidden.shape
    next_count = next_hidden.shape[1]
    depth, features = pieces[0].shape[0], whole_grads.shape[1]
    width = depth * features
    owners = [lax.rem(place[0] + RING - step, RING) for step in range(RING)]
    rows_load = pltpu.make_async_copy(row_pair, rows_held, rows_arrived.at[0])
    rows_load.start()
    stores = [
        pltpu.make_async_copy(
            piece.at[:, features : 2 * features], whole_grads.at[pl.ds(owners[step] * depth, depth)], left.at[step]
        )
        for step, piece in enumerate(pieces)
    ]
    for store in stores:
        store.start()

    for step, piece in enumerate(pieces):
        block = piece[:, features : 2 * features].reshape(width, count)
        for start in range(0, width, BAND):
            size = min(BAND, width - start)
            part = block[start : start + size]
            high, low = split(dot(band[:size, :size], part) + dot(band[:size, BAND : BAND + size], part))
            row = slice(step * width + start, step * width + start + size)
            grads[row, :count] = high
            grads[row, count : 2 * count] = low
            grads[row, 2 * count :] = high

    feature_blocks = []
    for piece in pieces:
        packed = piece[:, 2 * features :].astype(F32)
        blocks = []
        for d in range(depth):
            blocks += [packed[d, :, :next_count], packed[d, :, next_count:]]
        nexts = jnp.concatenate(blocks, axis=0).astype(BF16)
        feature_blocks.append(jnp.concatenate([piece[:, :features].reshape(width, count), nexts], axis=1))
    turned = ring_swiglu(feature_blocks, gate_held, up_held)
    units[...] = turned[:, :count]
    next_units[...] = turned[:, count:]
    for source, target in ((units, hidden), (next_units, next_hidden)):
        stores.append(pltpu.make_async_copy(source, target, left.at[len(stores)]))
        stores[-1].start()
    turned = turned[:, :count].T
    rows_load.wait()
    high, low = split(dot(turned, rows_held[:rows]) + dot(turned, rows_held[2 * HALF : 2 * HALF + rows]))
    factor[:count] = high
    factor[count : 2 * count] = high
    factor[2 * count :] = low

    for step in range(RING):
        total[...] = dot(grads[step * width : (step + 1) * width], factor[...])
        for k in range(width // TILE):
            tile = owners[step] * (width // TILE) + k
            row = pl.ds(tile, 1)
            spots = offsets[place[1], row, :]
            coefficients[row, :] = picked(total[k * TILE : (k + 1) * TILE], spots) + momentum_part[row, :]
    value = coefficients[...]
    packed_held[...] = jnp.concatenate([value[:, : HALF // 2], value[:, HALF // 2 :]], axis=0).astype(BF16)
    for target in [sent.at[r] for r in range(sent.shape[0])]:
        stores.append(pltpu.make_async_copy(packed_held, target, left.at[len(stores)]))
        stores[-1].start()
    for store in stores:
        store.wait()


def next_kernel(next_hidden, down, row_pair, base, factor, down_held, base_held, down_arrived, base_left):
    rows = down.shape[0]
    bands = down_held.shape[0]
    span = down_held.shape[2]
    loads = [
        pltpu.make_async_copy(down.at[:, pl.ds(step * span, span)], down_held.at[step], down_arrived.at[step])
        for step in range(bands)
    ]
    for load in loads:
        load.start()
    turned = next_hidden[...].T
    along = (dot(turned, row_pair[:rows]) + dot(turned, row_pair[2 * HALF : 2 * HALF + rows])).T
    factor[...] = jnp.concatenate(split(along), axis=1)
    for step, load in enumerate(loads):
        load.wait()
        base_held[:, step * span : (step + 1) * span] = dot(turned, down_held[step])
    store = pltpu.make_async_copy(base_held, base.at[: turned.shape[0]], base_left.at[0])
    store.start()
    store.wait()


def output_kernel(
    values, offsets, next_rows, base_whole, back, out,
    base, dense, across, rearranged, columns, even_values, odd_values, base_arrived,
):
    replicas, tile_cols, _ = offsets.shape
    tokens = base.shape[0]
    base_load = pltpu.make_async_copy(base_whole.at[:tokens], base, base_arrived.at[0])
    base_load.start()
    bands = base.shape[1] // BAND
    chunks = base.shape[1] // 128
    for r in range(replicas):
        value = values[r].astype(F32)
        value = jnp.concatenate([value[:tile_cols], value[tile_cols:]], axis=1)
        columns[r] = (offsets[r] & (TILE - 1)).astype(F32)
        even_values[r] = jnp.where(offsets[r] < TILE, value, 0.0)
        odd_values[r] = jnp.where(offsets[r] < TILE, 0.0, value)
    place = lax.broadcasted_iota(jnp.int32, (TILE, 128), 0).astype(F32).astype(BF16)
    zero = jnp.zeros((PACK, 128), BF16)

    def one(tile, carry):
        for start in range(0, HALF, 128):
            listed = []
            for r in range(replicas):
                rows = (table[r, pl.ds(tile, 1), :][:, start : start + 128] for table in (columns, even_values, odd_values))
                listed.append([jnp.broadcast_to(row, (PACK, 128)).astype(BF16) for row in rows])
            for first in range(0, TILE, PACK):
                even, odd = zero, zero
                for spots, even_value, odd_value in listed:
                    hit = spots == place[first : first + PACK]
                    even += jnp.where(hit, even_value, zero)
                    odd += jnp.where(hit, odd_value, zero)
                row = pl.ds(pl.multiple_of(tile * TILE + first, PACK), PACK)
                dense[row, start : start + 128] = even
                dense[row, HALF + start : HALF + start + 128] = odd
        return carry

    lax.fori_loop(0, tile_cols, one, 0)
    for step in range(0, bands, 2):
        both = dot(dense[step * BAND : (step + 2) * BAND], next_rows[...]).astype(BF16)
        for k in range(2):
            part = both[k * BAND : (k + 1) * BAND]
            across[:BAND, (step + k) * 128 : (step + k + 1) * 128] = part
            across[BAND:, (step + k) * 128 : (step + k + 1) * 128] = part
    change = dot(back[...], across[...])
    base_load.wait()
    for step in range(bands):
        turned = change[:, step * 128 : (step + 1) * 128].T
        result = base[:, step * BAND : (step + 1) * BAND] - (STEP_RATE / replicas) * (turned[:tokens] + turned[tokens:])
        for c in range(BAND // 128):
            rearranged[pl.ds(step * (BAND // 128) + c, tokens, stride=chunks), :] = result[:, c * 128 : (c + 1) * 128]
    out[...] = rearranged[...].astype(BF16)


def kept_kernel(
    place, sent, offsets, whole_grads, hidden, momentum, row_pair, back, out,
    own, cotangent, held, ready, dense, left, right, incoming, outgoing, grads_arrived,
):
    steps, rows, span = held.shape
    spectral = 2 * HALF

    def load(step):
        return pltpu.make_async_copy(momentum.at[0, :, pl.ds(step * span, span)], held.at[step], incoming.at[step])

    def store(step):
        return pltpu.make_async_copy(ready.at[step], out.at[0, :, pl.ds(step * span, span)], outgoing.at[step])

    grads_load = pltpu.make_async_copy(whole_grads.at[: cotangent.shape[0]], cotangent, grads_arrived.at[0])
    grads_load.start()
    for step in range(steps):
        load(step).start()
    value = sent[0].astype(F32)
    own[...] = jnp.concatenate([value[: own.shape[0]], value[own.shape[0] :]], axis=1)
    left[:, :spectral] = row_pair[:rows]
    left[:, spectral : 2 * spectral] = row_pair[:rows]
    left[:, 2 * spectral : 3 * spectral] = row_pair[spectral : spectral + rows]
    left[:, 3 * spectral :] = -hidden[...]
    column = lax.broadcasted_iota(jnp.int32, (TILE, HALF), 0)
    grads_load.wait()
    grads = cotangent[...].reshape(steps * span, cotangent.shape[2])
    for step in range(steps):
        for start in range(0, span, BAND):
            for k in range(BAND // TILE):
                tile = (step * span + start) // TILE + k
                spots, value = offsets[place[1], tile : tile + 1, :], own[tile : tile + 1, :]
                even = jnp.where(spots == column, value, 0.0).astype(BF16)
                odd = jnp.where(spots == column + TILE, value, 0.0).astype(BF16)
                for copy in range(2):
                    dense[copy * BAND + k * TILE : copy * BAND + (k + 1) * TILE, :HALF] = even
                    dense[copy * BAND + k * TILE : copy * BAND + (k + 1) * TILE, HALF:] = odd
            high, low = split(dot(back[...], dense[...]))
            right[start : start + BAND, :spectral] = high
            right[start : start + BAND, spectral : 2 * spectral] = low
            right[start : start + BAND, 2 * spectral : 3 * spectral] = high
        right[:, 3 * spectral :] = grads[step * span : (step + 1) * span]
        change = dot_turned(left[...], right[...])
        load(step).wait()
        ready[step] = (BETA_DECAY * held[step].astype(F32) - change).astype(BF16)
        store(step).start()
    for step in range(steps):
        store(step).wait()


def sum_kernel(received, out):
    total = jnp.sum(received[...].astype(F32), axis=0)
    chunks = out.shape[1] // 128
    lines = [
        jnp.concatenate([total[h * chunks + c : h * chunks + c + 1] for c in range(chunks)], axis=1)
        for h in range(out.shape[0])
    ]
    out[...] = jnp.concatenate(lines, axis=0).astype(BF16)


IN_VMEM = pl.BlockSpec(memory_space=pltpu.VMEM)
IN_SMEM = pl.BlockSpec(memory_space=pltpu.SMEM)
IN_HBM = pl.BlockSpec(memory_space=pltpu.HBM)


def params(limit=36):
    return pltpu.CompilerParams(vmem_limit_bytes=limit * 1024 * 1024)


def cost(flops, moved):
    return pl.CostEstimate(flops=int(flops), bytes_accessed=int(moved), transcendentals=0)


def depth_gather(block, depth):
    groups = [[x * depth + z for z in range(depth)] for x in range(RING)]
    return lax.all_to_all(block, "tensor", 0, 0, tiled=True, axis_index_groups=groups)


def ring_gather(block, depth):
    pieces = [block]
    for step in range(1, RING):
        pairs = [(x * depth + z, (x + step) % RING * depth + z) for x in range(RING) for z in range(depth)]
        pieces.append(lax.ppermute(block, "tensor", pairs))
    return pieces


def on_device(tokens, next_tokens, cotangent, gate_weight, up_weight, down_weight, momentum, indices):
    shards = lax.axis_size("tensor")
    depth = shards // RING
    replicas = lax.axis_size("replica")
    place = jnp.stack([lax.axis_index("tensor") // depth, lax.axis_index("replica")]).astype(jnp.int32)
    rows, width = down_weight.shape
    bands = width // BAND
    part = width // RING
    tile_rows, tile_cols, keep = indices.shape[1:]
    stride = TILE * TILE // keep
    count, next_count, features = tokens.shape[0], next_tokens.shape[0], tokens.shape[1]
    row_pair = jnp.asarray(np.concatenate(parts(row_table(rows))))
    band = jnp.asarray(np.concatenate(parts(band_table()), axis=1))
    back = jnp.asarray(np.concatenate(parts(band_table().T), axis=1))
    gate, up = gate_weight.T, up_weight.T

    packed = pl.pallas_call(
        pack_kernel,
        in_specs=[IN_VMEM] * 3,
        out_specs=IN_VMEM,
        out_shape=jax.ShapeDtypeStruct((depth, 2 * features + features // 2, count), BF16),
        compiler_params=params(58),
        name="pack",
    )(tokens.T, cotangent.T, next_tokens)
    pieces = ring_gather(depth_gather(packed, depth), depth)

    offsets = indices - jnp.arange(keep, dtype=jnp.int32) * stride
    offsets = offsets.transpose(0, 2, 1, 3).reshape(replicas, tile_cols, tile_rows * keep)
    offsets = jnp.pad(offsets, ((0, 0), (0, 0), (0, HALF - tile_rows * keep)), constant_values=-1)

    def shape(dims, kind):
        return jax.ShapeDtypeStruct(dims, kind)

    dma = pltpu.SemaphoreType.DMA

    momentum_part, gate_held, up_held = pl.pallas_call(
        momentum_pick_kernel,
        in_specs=[IN_SMEM] + [IN_HBM] * 3 + [IN_VMEM] * 3,
        out_specs=[IN_VMEM] * 3,
        out_shape=[shape((tile_cols, HALF), F32)] + [shape((RING, rows, part), BF16)] * 2,
        scratch_shapes=[
            pltpu.VMEM((width // SPAN, rows, SPAN), BF16),
            pltpu.VMEM((SPAN, 4 * HALF), BF16),
            pltpu.VMEM((3 * BAND, 2 * HALF), BF16),
            dma((width // SPAN,)),
            dma((2 * RING,)),
        ],
        compiler_params=params(36),
        cost_estimate=cost(6e9, 8e6),
        name="momentum_pick",
    )(place, momentum, gate, up, row_pair, band, offsets)

    whole_grads, hidden, next_hidden, sent = pl.pallas_call(
        pick_kernel,
        in_specs=[IN_SMEM] + [IN_VMEM] * (RING + 2) + [IN_HBM] + [IN_VMEM] * 3,
        out_specs=[IN_HBM] * 4,
        out_shape=[
            shape((ROOM // (features * count * 2), features, count), BF16),
            shape((rows, count), BF16),
            shape((rows, next_count), BF16),
            shape((replicas, 2 * tile_cols, HALF // 2), BF16),
        ],
        scratch_shapes=[
            pltpu.VMEM((width, 3 * count), BF16),
            pltpu.VMEM((part, 2 * HALF), F32),
            pltpu.VMEM((3 * count, 2 * HALF), BF16),
            pltpu.VMEM((4 * HALF, 2 * HALF), BF16),
            pltpu.VMEM((rows, count), BF16),
            pltpu.VMEM((rows, next_count), BF16),
            pltpu.VMEM((tile_cols, HALF), F32),
            pltpu.VMEM((2 * tile_cols, HALF // 2), BF16),
            dma((1,)),
            dma((RING + 2 + replicas,)),
        ],
        compiler_params=params(36),
        cost_estimate=cost(6e9, 12e6),
        name="pick",
    )(place, *pieces, gate_held, up_held, row_pair, band, momentum_part, offsets)

    listed = lax.all_to_all(sent, "replica", 0, 0, tiled=True)

    base, next_rows = pl.pallas_call(
        next_kernel,
        in_specs=[IN_VMEM, IN_HBM, IN_VMEM],
        out_specs=[IN_HBM, IN_VMEM],
        out_shape=[shape((ROOM // (width * 4), width), F32), shape((2 * HALF, 2 * next_count), BF16)],
        scratch_shapes=[
            pltpu.VMEM((width // SPAN, rows, SPAN), BF16),
            pltpu.VMEM((next_count, width), F32),
            dma((width // SPAN,)),
            dma((1,)),
        ],
        compiler_params=params(),
        cost_estimate=cost(2e9, 7e6),
        name="next_rows",
    )(next_hidden, down_weight, row_pair)

    partial = pl.pallas_call(
        output_kernel,
        in_specs=[IN_VMEM] * 3 + [IN_HBM, IN_VMEM],
        out_specs=IN_VMEM,
        out_shape=shape((next_count * width // 128, 128), BF16),
        scratch_shapes=[
            pltpu.VMEM((next_count, width), F32),
            pltpu.VMEM((width, 2 * HALF), BF16),
            pltpu.VMEM((2 * BAND, bands * 2 * next_count), BF16),
            pltpu.VMEM((next_count * width // 128, 128), F32),
        ]
        + [pltpu.VMEM((replicas, tile_cols, HALF), F32)] * 3
        + [dma((1,))],
        compiler_params=params(),
        cost_estimate=cost(4e9, 4e6),
        name="output_part",
    )(listed, offsets, next_rows, base, back)

    received = lax.all_to_all(partial.reshape(shards, -1, 128), "tensor", 0, 0, tiled=True)
    output = pl.pallas_call(
        sum_kernel,
        in_specs=[IN_VMEM],
        out_specs=IN_VMEM,
        out_shape=shape((next_count // shards, width), BF16),
        compiler_params=params(),
        name="output_sum",
    )(received)

    kept = pl.pallas_call(
        kept_kernel,
        in_specs=[IN_SMEM, IN_VMEM, IN_VMEM, IN_HBM, IN_VMEM, IN_HBM, IN_VMEM, IN_VMEM],
        out_specs=IN_HBM,
        out_shape=shape((1, rows, width), BF16),
        scratch_shapes=[pltpu.VMEM((tile_cols, HALF), F32), pltpu.VMEM((shards, features, count), BF16)]
        + [pltpu.VMEM((width // SPAN, rows, SPAN), BF16)] * 2
        + [
            pltpu.VMEM((2 * BAND, 2 * HALF), BF16),
            pltpu.VMEM((rows, 6 * HALF + count), BF16),
            pltpu.VMEM((SPAN, 6 * HALF + count), BF16),
            dma((width // SPAN,)),
            dma((width // SPAN,)),
            dma((1,)),
        ],
        compiler_params=params(),
        cost_estimate=cost(10e9, 8e6),
        name="kept",
    )(place, sent, offsets, whole_grads, hidden, momentum, row_pair, back)
    return (output, kept)


def solution(mesh):
    return jax.shard_map(
        on_device,
        mesh=mesh,
        in_specs=(
            P("replica", "tensor"),
            P("replica", "tensor"),
            P("replica", "tensor"),
            P(None, "tensor"),
            P(None, "tensor"),
            P("tensor", None),
            P("replica", "tensor", None),
            P(None, "tensor", None, None),
        ),
        out_specs=(P(("replica", "tensor"), None), P("replica", "tensor", None)),
        check_vma=False,
    )
```

time: 96.6 us -> 90.1 us (0.933)
  Pallas kernels: 43.1 us -> 34.2 us
  local copies, waits for them, and re-layouts: 5.97 us -> 11.8 us
  starting transfers between devices: 28.7 us -> 25.3 us
    pallas_call x5 -> x7, Pallas kernels: 43.1 us -> 34.2 us  [the longest x1 10.8 us: on_device(): pl.pallas_call(kept_kernel, in_specs=[IN_SMEM, IN_VMEM, IN_VMEM, IN_HBM,...]
    unnamed x19 -> x22, local copies, waits for them, and re-layouts: 3.44 us -> 8.62 us
    all_to_all x1, waiting for transfers between devices: 3.96 us -> 8 us  [depth_gather(): lax.all_to_all(block, 'tensor', 0, 0, tiled=True, axis_index_groups=groups)]
    ppermute x6 -> x3, starting transfers between devices: 8.03 us -> 4.44 us  [ring_gather(): pieces.append(lax.ppermute(block, 'tensor', pairs))]
    ppermute x6 -> x3, waiting for transfers between devices: 7.42 us -> 4.13 us  [ring_gather(): pieces.append(lax.ppermute(block, 'tensor', pairs))]
    all_to_all x1, waiting for transfers between devices: 4.23 us -> 1.71 us  [on_device(): lax.all_to_all(partial.reshape(shards, -1, 128), 'tensor', 0, 0, tiled=True)]
    sub x1, other arithmetic: 0.17 us -> 2.28 us  [on_device(): offsets = indices - jnp.arange(keep, dtype=jnp.int32) * stride]
    reshape x1, local copies, waits for them, and re-layouts: 0.31 us -> 2.2 us  [on_device(): offsets.transpose(0, 2, 1, 3).reshape(replicas, tile_cols, tile_rows * keep)]
  transfers between devices with their start and end apart: 9 -> 6, of which waited for: 4 -> 5; matrix products, arithmetic and copies ran while one was open for 2% -> 6% of each run, Pallas kernels for 39% -> 23%
where the time goes in v3:
time: 90.1 us; the launch traced here: 89.3 us
  Pallas kernels  34.2 us (38%)
  starting transfers between devices  25.3 us (28%)
  waiting for transfers between devices  14.9 us (17%)
  local copies, waits for them, and re-layouts  11.8 us (13%)
  other arithmetic  2.36 us (3%)
    pallas_call x1, Pallas kernels, on_device(): pl.pallas_call(kept_kernel, in_specs=[IN_SMEM, IN_VMEM, IN_VMEM, IN_HBM,...  10.8 us
    all_to_all x1, starting transfers between devices, depth_gather(): lax.all_to_all(block, 'tensor', 0, 0, tiled=True, axis_index_groups=groups)  8.7 us
    unnamed x22, local copies, waits for them, and re-layouts  8.62 us
    all_to_all x1, waiting for transfers between devices, depth_gather(): lax.all_to_all(block, 'tensor', 0, 0, tiled=True, axis_index_groups=groups)  8 us
    all_to_all x1, starting transfers between devices, on_device(): lax.all_to_all(partial.reshape(shards, -1, 128), 'tensor', 0, 0, tiled=True)  7.67 us
    pallas_call x1, Pallas kernels, on_device(): pl.pallas_call(momentum_pick_kernel, in_specs=[IN_SMEM] + [IN_HBM] * 3 +...  7.6 us
    pallas_call x1, Pallas kernels, on_device(): pl.pallas_call(pick_kernel, in_specs=[IN_SMEM] + [IN_VMEM] * (RING + 2) +...  5.89 us
    pallas_call x1, Pallas kernels, on_device(): pl.pallas_call(output_kernel, in_specs=[IN_VMEM] * 3 + [IN_HBM, IN_VMEM],...  5.01 us
  transfers between devices with their start and end apart: 6, of which 5 were waited for; matrix products, arithmetic and copies ran while one was open for 6% of the time, Pallas kernels for 23%

profile of v3, /device:TPU:32, one launch (start us, length us, event | category | flops | bytes accessed | tf_op | source)
XLA Modules:
  0.0 89.3 jit_solution(16003781111674919061)
XLA Ops:
  0.6 1.7 %pack.1 = bf16[8,200,128]{2,1,0:T(8,128)(2,1)} custom-call(bf16[80,128]{1,0:T(8,128)(2,1)} %bitcast.13, bf16[80,128]{1,0:T(8,128)(2,1)} %bitcast.14, bf16[64,80]{1,0:T(8,128)(2,1)} %next_tokens.1), custom_call_target="tpu_custom_call" | custom-call | tf_op jit(solution)/shard_map/pack/pallas_call | solution.py:378
  2.3 0.0 copy-start
  2.3 0.0 copy-start.9
  2.3 8.7 %all-to-all-start = ((bf16[8,200,128]{2,1,0:T(8,128)(2,1)}), bf16[8,200,128]{2,1,0:T(8,128)(2,1)S(1)}, u32[]{:S(2)}, u32[]{:S(2)}) async-start(bf16[8,200,128]{2,1,0:T(8,128)(2,1)} %pack.1), calls=%async_computation | async-start | bytes 819200 | tf_op jit(solution)/shard_map/all_to_all | solution.py:351
  11.0 2.3 %broadcast_subtract_fusion = s32[8,7,40,32]{2,3,1,0:T(8,128)} fusion(s32[8,7,40,32]{2,3,1,0:T(8,128)} %param.18, s32[32]{0:T(128)S(1)} %iota_multiply_fusion), kind=kLoop, calls=%fused_computation | loop fusion | flops 71680 | bytes 573568 | tf_op jit(solution)/shard_map/sub | solution.py:388
  13.3 2.2 %copy.15 = s32[8,40,224]{2,1,0:T(8,128)} copy(s32[8,40,224]{1,2,0:T(8,128)} %bitcast.12) | data formatting | bytes 573440 | tf_op jit(solution)/shard_map/reshape | solution.py:389
  15.5 1.0 %pad.4.offsets.refs_9_ = s32[8,40,256]{2,1,0:T(8,128)S(1)} pad(s32[8,40,224]{2,1,0:T(8,128)} %copy.15, s32[]{:T(128)} %constant.30.clone.1), padding=0_0x0_0x0_32 | pad | bytes 614404 | tf_op jit(solution)/shard_map/jit(_pad)/pad | solution.py:390
  16.5 0.1 pad_add_fusion.place
  16.6 8.0 %all-to-all-done.refs_0_ = bf16[8,200,128]{2,1,0:T(8,128)(2,1)S(1)} async-done(((bf16[8,200,128]{2,1,0:T(8,128)(2,1)}), bf16[8,200,128]{2,1,0:T(8,128)(2,1)S(1)}, u32[]{:S(2)}, u32[]{:S(2)}) %all-to-all-start) | async-done | bytes 409632 | tf_op jit(solution)/shard_map/all_to_all | solution.py:351
  24.6 2.8 %collective-permute-start.2 = (bf16[8,200,128]{2,1,0:T(8,128)(2,1)S(1)}, bf16[8,200,128]{2,1,0:T(8,128)(2,1)S(1)}, u32[]{:S(2)}, u32[]{:S(2)}) collective-permute-start(bf16[8,200,128]{2,1,0:T(8,128)(2,1)S(1)} %all-to-all-done.refs_0_), channel_id=1, source_target_pairs={{0,24},{1,25},{2,26},{3,27},{4,28},{5,29},{6,30},{7,31},{8,0},{9,1... | collective-permute-start | bytes 1228808 | tf_op jit(solution)/shard_map/ppermute | solution.py:358
  27.3 0.8 collective-permute-start.1
  28.1 0.9 collective-permute-start
  29.0 0.0 copy-done
  29.0 0.0 copy-done.9
  29.0 0.0 copy-start.2
  29.0 1.2 %copy-done.2 = bf16[1024,512]{1,0:T(8,128)(2,1)S(1)} copy-done((bf16[1024,512]{1,0:T(8,128)(2,1)S(1)}, bf16[1024,512]{1,0:T(8,128)(2,1)}, u32[]{:S(2)}) %copy-start.2) | copy-done | bytes 1048600
  30.3 0.0 copy-start.6
  30.3 1.6 %copy-done.6 = bf16[2560,448]{0,1:T(8,128)(2,1)S(1)} copy-done((bf16[2560,448]{0,1:T(8,128)(2,1)S(1)}, bf16[2560,448]{0,1:T(8,128)(2,1)}, u32[]{:S(2)}) %copy-start.6) | copy-done | bytes 2293784
  31.9 0.0 copy-start.7
  31.9 1.6 %copy-done.7 = bf16[2560,448]{0,1:T(8,128)(2,1)S(1)} copy-done((bf16[2560,448]{0,1:T(8,128)(2,1)S(1)}, bf16[2560,448]{0,1:T(8,128)(2,1)}, u32[]{:S(2)}) %copy-start.7) | copy-done | bytes 2293784
  33.6 0.0 copy-start.3
  33.6 0.0 copy-start.10
  33.6 7.6 %momentum_pick.1 = (f32[40,256]{1,0:T(8,128)S(1)}, bf16[4,448,640]{2,1,0:T(8,128)(2,1)S(1)}, bf16[4,448,640]{2,1,0:T(8,128)(2,1)S(1)}) custom-call(s32[2]{0:T(128)S(1)} %pad_add_fusion.place, bf16[1,448,2560]{2,1,0:T(8,128)(2,1)S(1)} %copy-done, bf16[448,2560]{1,0:T(8,128)(2,1)S(1)} %bitcast.10, bf16[448,2560]{1,0:T(8,128)(2,1)S(1)} %bitcast.11, ...), custom_call_target="tpu_custom_call" | custom-call | flops 6000000000 | bytes 8000000 | tf_op jit(solution)/shard_map/momentum_pick/pallas_call | solution.py:397
  41.2 0.4 collective-permute-done.2.refs_3_
  41.6 0.0 collective-permute-done.1.refs_2_
  41.6 3.7 %collective-permute-done.refs_1_ = bf16[8,200,128]{2,1,0:T(8,128)(2,1)S(1)} collective-permute-done((bf16[8,200,128]{2,1,0:T(8,128)(2,1)S(1)}, bf16[8,200,128]{2,1,0:T(8,128)(2,1)S(1)}, u32[]{:S(2)}, u32[]{:S(2)}) %collective-permute-start) | collective-permute-done | bytes 409632 | tf_op jit(solution)/shard_map/ppermute | solution.py:358
  45.3 0.0 copy-done.3
  45.3 0.0 copy-done.10
  45.3 5.9 %pick.1 = (bf16[1638,80,128]{2,1,0:T(8,128)(2,1)}, bf16[448,128]{1,0:T(8,128)(2,1)S(1)}, bf16[448,64]{1,0:T(8,128)(2,1)S(1)}, bf16[8,80,128]{2,1,0:T(8,128)(2,1)}) custom-call(s32[2]{0:T(128)S(1)} %pad_add_fusion.place, bf16[8,200,128]{2,1,0:T(8,128)(2,1)S(1)} %all-to-all-done.refs_0_, bf16[8,200,128]{2,1,0:T(8,128)(2,1)S(1)} %collective-permute-done.refs_1_, ...), custom_call_target="tpu_custom_call" | custom-call | flops 6000000000 | bytes 12000000 | tf_op jit(solution)/shard_map/pick/pallas_call | solution.py:414
  51.2 4.5 %all-to-all-start.1 = ((bf16[8,80,128]{2,1,0:T(8,128)(2,1)}), bf16[8,80,128]{2,1,0:T(8,128)(2,1)S(1)}, u32[]{:S(2)}, u32[]{:S(2)}) async-start(bf16[8,80,128]{2,1,0:T(8,128)(2,1)} %get-tuple-element.14.sent), calls=%async_computation.1 | async-start | bytes 327680 | tf_op jit(solution)/shard_map/all_to_all | solution.py:441
  55.7 0.0 copy-start.4
  55.7 1.2 %copy-done.4 = bf16[1024,512]{1,0:T(8,128)(2,1)S(1)} copy-done((bf16[1024,512]{1,0:T(8,128)(2,1)S(1)}, bf16[1024,512]{1,0:T(8,128)(2,1)}, u32[]{:S(2)}) %copy-start.4) | copy-done | bytes 1048600
  56.9 0.0 copy-start.8
  56.9 1.6 %copy-done.8 = bf16[448,2560]{1,0:T(8,128)(2,1)S(1)} copy-done((bf16[448,2560]{1,0:T(8,128)(2,1)S(1)}, bf16[448,2560]{1,0:T(8,128)(2,1)}, u32[]{:S(2)}) %copy-start.8) | copy-done | bytes 2293784
  58.6 0.0 copy-start.1
  58.6 2.6 %next_rows.1 = (f32[3276,2560]{1,0:T(8,128)}, bf16[512,128]{1,0:T(8,128)(2,1)S(1)}) custom-call(bf16[448,64]{1,0:T(8,128)(2,1)S(1)} %get-tuple-element.15.next_hidden, bf16[448,2560]{1,0:T(8,128)(2,1)S(1)} %copy-done.8, bf16[1024,512]{1,0:T(8,128)(2,1)S(1)} %copy-done.4), custom_call_target="tpu_custom_call" | custom-call | flops 2000000000 | bytes 7000000 | tf_op jit(solution)/shard_map/next_rows/pallas_call | solution.py:443
  61.1 1.0 %all-to-all-done.1.values = bf16[8,80,128]{2,1,0:T(8,128)(2,1)S(1)} async-done(((bf16[8,80,128]{2,1,0:T(8,128)(2,1)}), bf16[8,80,128]{2,1,0:T(8,128)(2,1)S(1)}, u32[]{:S(2)}, u32[]{:S(2)}) %all-to-all-start.1) | async-done | bytes 163872 | tf_op jit(solution)/shard_map/all_to_all | solution.py:441
  62.2 0.0 copy-done.1
  62.2 5.0 %output_part.1 = bf16[1280,128]{1,0:T(8,128)(2,1)} custom-call(bf16[8,80,128]{2,1,0:T(8,128)(2,1)S(1)} %all-to-all-done.1.values, s32[8,40,256]{2,1,0:T(8,128)S(1)} %pad.4.offsets.refs_9_, bf16[512,128]{1,0:T(8,128)(2,1)S(1)} %get-tuple-element.16.next_rows, f32[3276,2560]{1,0:T(8,128)} %get-tuple-element.17.base_whole, bf16[256,512]{1,0:T(8,128)(2,1)S(1)} %copy-done.1), custom_call_target="tpu_custom_call" | custom-call | flops 4000000000 | bytes 4000000 | tf_op jit(solution)/shard_map/output_part/pallas_call | solution.py:459
  67.2 7.7 %all-to-all-start.2 = ((bf16[32,40,128]{2,1,0:T(8,128)(2,1)}), bf16[32,40,128]{2,1,0:T(8,128)(2,1)S(1)}, u32[]{:S(2)}, u32[]{:S(2)}) async-start(bf16[32,40,128]{2,1,0:T(8,128)(2,1)} %bitcast.8), calls=%async_computation.2 | async-start | bytes 655360 | tf_op jit(solution)/shard_map/all_to_all | solution.py:477
  74.9 0.0 copy-start.5
  74.9 1.2 %copy-done.5 = bf16[1024,512]{1,0:T(8,128)(2,1)S(1)} copy-done((bf16[1024,512]{1,0:T(8,128)(2,1)S(1)}, bf16[1024,512]{1,0:T(8,128)(2,1)}, u32[]{:S(2)}) %copy-start.5) | copy-done | bytes 1048600
  76.1 10.8 %kept.1 = bf16[1,448,2560]{2,1,0:T(8,128)(2,1)} custom-call(s32[2]{0:T(128)S(1)} %pad_add_fusion.place, bf16[8,80,128]{2,1,0:T(8,128)(2,1)} %get-tuple-element.14.sent, s32[8,40,256]{2,1,0:T(8,128)S(1)} %pad.4.offsets.refs_9_, bf16[1638,80,128]{2,1,0:T(8,128)(2,1)} %get-tuple-element.18.whole_grads, bf16[448,128]{1,0:T(8,128)(2,1)S(1)} %get-tuple-element.19.hidden, ...), custom_call_target="tpu_custom_call" | custom-call | flops 10000000000 | bytes 8000000 | tf_op jit(solution)/shard_map/kept/pallas_call | solution.py:487
  86.9 1.7 %all-to-all-done.2.received = bf16[32,40,128]{2,1,0:T(8,128)(2,1)S(1)} async-done(((bf16[32,40,128]{2,1,0:T(8,128)(2,1)}), bf16[32,40,128]{2,1,0:T(8,128)(2,1)S(1)}, u32[]{:S(2)}, u32[]{:S(2)}) %all-to-all-start.2) | async-done | bytes 327712 | tf_op jit(solution)/shard_map/all_to_all | solution.py:477
  88.6 0.7 output_sum.1
  (1 shorter events, 0.0 us)
Async XLA Ops:
  2.3 26.7 %copy-start = (bf16[1,448,2560]{2,1,0:T(8,128)(2,1)S(1)}, bf16[1,448,2560]{2,1,0:T(8,128)(2,1)}, u32[]{:S(2)}) copy-start(bf16[1,448,2560]{2,1,0:T(8,128)(2,1)} %momentum.3) | copy-start | bytes 6881284
  2.3 26.7 %copy-start.9 = (bf16[256,512]{1,0:T(8,128)(2,1)S(1)}, bf16[256,512]{1,0:T(8,128)(2,1)}, u32[]{:S(2)}) copy-start(bf16[256,512]{1,0:T(8,128)(2,1)} %constant.35.clone.band.refs_7_) | copy-start | bytes 786436
  2.3 22.3 %all-to-all-start = ((bf16[8,200,128]{2,1,0:T(8,128)(2,1)}), bf16[8,200,128]{2,1,0:T(8,128)(2,1)S(1)}, u32[]{:S(2)}, u32[]{:S(2)}) async-start(bf16[8,200,128]{2,1,0:T(8,128)(2,1)} %pack.1), calls=%async_computation | async-start | bytes 819200 | tf_op jit(solution)/shard_map/all_to_all | solution.py:351
  24.6 17.0 %collective-permute-start.2 = (bf16[8,200,128]{2,1,0:T(8,128)(2,1)S(1)}, bf16[8,200,128]{2,1,0:T(8,128)(2,1)S(1)}, u32[]{:S(2)}, u32[]{:S(2)}) collective-permute-start(bf16[8,200,128]{2,1,0:T(8,128)(2,1)S(1)} %all-to-all-done.refs_0_), channel_id=1, source_target_pairs={{0,24},{1,25},{2,26},{3,27},{4,28},{5,29},{6,30},{7,31},{8,0},{9,1... | collective-permute-start | bytes 1228808 | tf_op jit(solution)/shard_map/ppermute | solution.py:358
  27.3 14.2 %collective-permute-start.1 = (bf16[8,200,128]{2,1,0:T(8,128)(2,1)S(1)}, bf16[8,200,128]{2,1,0:T(8,128)(2,1)S(1)}, u32[]{:S(2)}, u32[]{:S(2)}) collective-permute-start(bf16[8,200,128]{2,1,0:T(8,128)(2,1)S(1)} %all-to-all-done.refs_0_), channel_id=1, source_target_pairs={{0,16},{1,17},{2,18},{3,19},{4,20},{5,21},{6,22},{7,23},{8,24},{9,... | collective-permute-start | bytes 1228808 | tf_op jit(solution)/shard_map/ppermute | solution.py:358
  28.1 17.2 %collective-permute-start = (bf16[8,200,128]{2,1,0:T(8,128)(2,1)S(1)}, bf16[8,200,128]{2,1,0:T(8,128)(2,1)S(1)}, u32[]{:S(2)}, u32[]{:S(2)}) collective-permute-start(bf16[8,200,128]{2,1,0:T(8,128)(2,1)S(1)} %all-to-all-done.refs_0_), channel_id=1, source_target_pairs={{0,8},{1,9},{2,10},{3,11},{4,12},{5,13},{6,14},{7,15},{8,16},{9,17... | collective-permute-start | bytes 1228808 | tf_op jit(solution)/shard_map/ppermute | solution.py:358
  29.0 1.2 %copy-start.2 = (bf16[1024,512]{1,0:T(8,128)(2,1)S(1)}, bf16[1024,512]{1,0:T(8,128)(2,1)}, u32[]{:S(2)}) copy-start(bf16[1024,512]{1,0:T(8,128)(2,1)} %constant.34.clone.row_pair.refs_6_) | copy-start | bytes 3145732
  30.3 1.6 %copy-start.6 = (bf16[2560,448]{0,1:T(8,128)(2,1)S(1)}, bf16[2560,448]{0,1:T(8,128)(2,1)}, u32[]{:S(2)}) copy-start(bf16[2560,448]{0,1:T(8,128)(2,1)} %param.14) | copy-start | bytes 6881284
  31.9 1.6 %copy-start.7 = (bf16[2560,448]{0,1:T(8,128)(2,1)S(1)}, bf16[2560,448]{0,1:T(8,128)(2,1)}, u32[]{:S(2)}) copy-start(bf16[2560,448]{0,1:T(8,128)(2,1)} %param.15) | copy-start | bytes 6881284
  33.6 11.7 %copy-start.3 = (bf16[1024,512]{1,0:T(8,128)(2,1)S(1)}, bf16[1024,512]{1,0:T(8,128)(2,1)}, u32[]{:S(2)}) copy-start(bf16[1024,512]{1,0:T(8,128)(2,1)} %constant.34.clone.row_pair.refs_6_) | copy-start | bytes 3145732
  33.6 11.7 %copy-start.10 = (bf16[256,512]{1,0:T(8,128)(2,1)S(1)}, bf16[256,512]{1,0:T(8,128)(2,1)}, u32[]{:S(2)}) copy-start(bf16[256,512]{1,0:T(8,128)(2,1)} %constant.35.clone.band.refs_7_) | copy-start | bytes 786436
  51.2 11.0 %all-to-all-start.1 = ((bf16[8,80,128]{2,1,0:T(8,128)(2,1)}), bf16[8,80,128]{2,1,0:T(8,128)(2,1)S(1)}, u32[]{:S(2)}, u32[]{:S(2)}) async-start(bf16[8,80,128]{2,1,0:T(8,128)(2,1)} %get-tuple-element.14.sent), calls=%async_computation.1 | async-start | bytes 327680 | tf_op jit(solution)/shard_map/all_to_all | solution.py:441
  55.7 1.2 %copy-start.4 = (bf16[1024,512]{1,0:T(8,128)(2,1)S(1)}, bf16[1024,512]{1,0:T(8,128)(2,1)}, u32[]{:S(2)}) copy-start(bf16[1024,512]{1,0:T(8,128)(2,1)} %constant.34.clone.row_pair.refs_6_) | copy-start | bytes 3145732
  56.9 1.6 %copy-start.8 = (bf16[448,2560]{1,0:T(8,128)(2,1)S(1)}, bf16[448,2560]{1,0:T(8,128)(2,1)}, u32[]{:S(2)}) copy-start(bf16[448,2560]{1,0:T(8,128)(2,1)} %down.1) | copy-start | bytes 6881284
  58.6 3.6 %copy-start.1 = (bf16[256,512]{1,0:T(8,128)(2,1)S(1)}, bf16[256,512]{1,0:T(8,128)(2,1)}, u32[]{:S(2)}) copy-start(bf16[256,512]{1,0:T(8,128)(2,1)} %constant.36.clone.back) | copy-start | bytes 786436
  67.2 21.4 %all-to-all-start.2 = ((bf16[32,40,128]{2,1,0:T(8,128)(2,1)}), bf16[32,40,128]{2,1,0:T(8,128)(2,1)S(1)}, u32[]{:S(2)}, u32[]{:S(2)}) async-start(bf16[32,40,128]{2,1,0:T(8,128)(2,1)} %bitcast.8), calls=%async_computation.2 | async-start | bytes 655360 | tf_op jit(solution)/shard_map/all_to_all | solution.py:477
  74.9 1.2 %copy-start.5 = (bf16[1024,512]{1,0:T(8,128)(2,1)S(1)}, bf16[1024,512]{1,0:T(8,128)(2,1)}, u32[]{:S(2)}) copy-start(bf16[1024,512]{1,0:T(8,128)(2,1)} %constant.34.clone.row_pair.refs_6_) | copy-start | bytes 3145732

commit v4 on v3

--- a/solution.py
+++ b/solution.py
@@ -77,7 +77,8 @@
 
 
 def momentum_pick_kernel(
-    place, momentum, gate, up, row_pair, band, offsets, out, gate_held, up_held, held, twice, stack, incoming, arrived
+    place, momentum, gate, up, row_pair, band, offsets, piece, out, gate_held, up_held, gated, upper, grads,
+    held, twice, stack, incoming, arrived,
 ):
     steps, rows, span = held.shape
 
@@ -108,6 +109,36 @@
                 out[tile : tile + 1, :] = picked(total[k * TILE : (k + 1) * TILE], spots)
     for weight in weights:
         weight.wait()
+    feature = piece_features(piece, gated.shape[1])
+    gated[...] = dot(gate_held[0], feature)
+    upper[...] = dot(up_held[0], feature)
+    piece_grads(piece, band, grads)
+
+
+def piece_features(piece, columns):
+    depth, lines, count = piece.shape
+    features = 2 * lines // 5
+    next_count = columns - count
+    packed = piece[:, 2 * features :].astype(F32)
+    blocks = []
+    for d in range(depth):
+        blocks += [packed[d, :, :next_count], packed[d, :, next_count:]]
+    nexts = jnp.concatenate(blocks, axis=0).astype(BF16)
+    return jnp.concatenate([piece[:, :features].reshape(depth * features, count), nexts], axis=1)
+
+
+def piece_grads(piece, band, grads):
+    depth, lines, count = piece.shape
+    features = 2 * lines // 5
+    width = depth * features
+    block = piece[:, features : 2 * features].reshape(width, count)
+    for start in range(0, width, BAND):
+        size = min(BAND, width - start)
+        part = block[start : start + size]
+        high, low = split(dot(band[:size, :size], part) + dot(band[:size, BAND : BAND + size], part))
+        grads[start : start + size, :count] = high
+        grads[start : start + size, count : 2 * count] = low
+        grads[start : start + size, 2 * count :] = high
 
 
 def weight_loads(place, gate, up, gate_held, up_held, arrived):
@@ -121,19 +152,18 @@
     return loads
 
 
-def ring_swiglu(features, gate_held, up_held):
-    gated = upper = None
+def ring_swiglu(gated, upper, features, gate_held, up_held):
     for step, feature in enumerate(features):
-        term = dot(gate_held[step], feature)
-        gated = term if gated is None else gated + term
-        term = dot(up_held[step], feature)
-        upper = term if upper is None else upper + term
+        gated = gated + dot(gate_held[step + 1], feature)
+        upper = upper + dot(up_held[step + 1], feature)
     return (gated / (1.0 + jnp.exp(-gated)) * upper).astype(BF16)
 
 
 def pick_kernel(place, *refs):
     pieces = refs[:RING]
     gate_held, up_held, row_pair, band, momentum_part, offsets = refs[RING : RING + 6]
+    own_gated, own_upper, own_grads = refs[RING + 6 : RING + 9]
+    refs = refs[3:]
     whole_grads, hidden, next_hidden, sent = refs[RING + 6 : RING + 10]
     grads, total, factor, rows_held, units, next_units, coefficients, packed_held, rows_arrived, left = refs[RING + 10 :]
     rows, count = hidden.shape
@@ -152,26 +182,11 @@
     for store in stores:
         store.start()
 
-    for step, piece in enumerate(pieces):
-        block = piece[:, features : 2 * features].reshape(width, count)
-        for start in range(0, width, BAND):
-            size = min(BAND, width - start)
-            part = block[start : start + size]
-            high, low = split(dot(band[:size, :size], part) + dot(band[:size, BAND : BAND + size], part))
-            row = slice(step * width + start, step * width + start + size)
-            grads[row, :count] = high
-            grads[row, count : 2 * count] = low
-            grads[row, 2 * count :] = high
-
-    feature_blocks = []
-    for piece in pieces:
-        packed = piece[:, 2 * features :].astype(F32)
-        blocks = []
-        for d in range(depth):
-            blocks += [packed[d, :, :next_count], packed[d, :, next_count:]]
-        nexts = jnp.concatenate(blocks, axis=0).astype(BF16)
-        feature_blocks.append(jnp.concatenate([piece[:, :features].reshape(width, count), nexts], axis=1))
-    turned = ring_swiglu(feature_blocks, gate_held, up_held)
+    for step, piece in enumerate(pieces[1:]):
+        piece_grads(piece, band, grads.at[step * width : (step + 1) * width])
+    columns = count + next_count
+    feature_blocks = [piece_features(piece, columns) for piece in pieces[1:]]
+    turned = ring_swiglu(own_gated[...], own_upper[...], feature_blocks, gate_held, up_held)
     units[...] = turned[:, :count]
     next_units[...] = turned[:, count:]
     for source, target in ((units, hidden), (next_units, next_hidden)):
@@ -185,7 +200,8 @@
     factor[2 * count :] = low
 
     for step in range(RING):
-        total[...] = dot(grads[step * width : (step + 1) * width], factor[...])
+        part = own_grads[...] if step == 0 else grads[(step - 1) * width : step * width]
+        total[...] = dot(part, factor[...])
         for k in range(width // TILE):
             tile = owners[step] * (width // TILE) + k
             row = pl.ds(tile, 1)
@@ -257,7 +273,7 @@
                 dense[row, HALF + start : HALF + start + 128] = odd
         return carry
 
-    lax.fori_loop(0, tile_cols, one, 0)
+    lax.fori_loop(0, tile_cols, one, 0, unroll=4)
     for step in range(0, bands, 2):
         both = dot(dense[step * BAND : (step + 2) * BAND], next_rows[...]).astype(BF16)
         for k in range(2):
@@ -394,11 +410,14 @@
 
     dma = pltpu.SemaphoreType.DMA
 
-    momentum_part, gate_held, up_held = pl.pallas_call(
+    momentum_part, gate_held, up_held, *own_parts = pl.pallas_call(
         momentum_pick_kernel,
-        in_specs=[IN_SMEM] + [IN_HBM] * 3 + [IN_VMEM] * 3,
-        out_specs=[IN_VMEM] * 3,
-        out_shape=[shape((tile_cols, HALF), F32)] + [shape((RING, rows, part), BF16)] * 2,
+        in_specs=[IN_SMEM] + [IN_HBM] * 3 + [IN_VMEM] * 4,
+        out_specs=[IN_VMEM] * 6,
+        out_shape=[shape((tile_cols, HALF), F32)]
+        + [shape((RING, rows, part), BF16)] * 2
+        + [shape((rows, count + next_count), F32)] * 2
+        + [shape((part, 3 * count), BF16)],
         scratch_shapes=[
             pltpu.VMEM((width // SPAN, rows, SPAN), BF16),
             pltpu.VMEM((SPAN, 4 * HALF), BF16),
@@ -409,11 +428,11 @@
         compiler_params=params(36),
         cost_estimate=cost(6e9, 8e6),
         name="momentum_pick",
-    )(place, momentum, gate, up, row_pair, band, offsets)
+    )(place, momentum, gate, up, row_pair, band, offsets, pieces[0])
 
     whole_grads, hidden, next_hidden, sent = pl.pallas_call(
         pick_kernel,
-        in_specs=[IN_SMEM] + [IN_VMEM] * (RING + 2) + [IN_HBM] + [IN_VMEM] * 3,
+        in_specs=[IN_SMEM] + [IN_VMEM] * (RING + 2) + [IN_HBM] + [IN_VMEM] * 6,
         out_specs=[IN_HBM] * 4,
         out_shape=[
             shape((ROOM // (features * count * 2), features, count), BF16),
@@ -422,7 +441,7 @@
             shape((replicas, 2 * tile_cols, HALF // 2), BF16),
         ],
         scratch_shapes=[
-            pltpu.VMEM((width, 3 * count), BF16),
+            pltpu.VMEM((width - part, 3 * count), BF16),
             pltpu.VMEM((part, 2 * HALF), F32),
             pltpu.VMEM((3 * count, 2 * HALF), BF16),
             pltpu.VMEM((4 * HALF, 2 * HALF), BF16),
@@ -436,7 +455,7 @@
         compiler_params=params(36),
         cost_estimate=cost(6e9, 12e6),
         name="pick",
-    )(place, *pieces, gate_held, up_held, row_pair, band, momentum_part, offsets)
+    )(place, *pieces, gate_held, up_held, row_pair, band, momentum_part, offsets, *own_parts)
 
     listed = lax.all_to_all(sent, "replica", 0, 0, tiled=True)
 

time: 90.1 us -> 89.3 us (level)
  transfers between devices with their start and end apart: 6 -> 6, of which waited for: 5 -> 4; matrix products, arithmetic and copies ran while one was open for 6% -> 6% of each run, Pallas kernels for 23% -> 25%
where the time goes in v4:
time: 89.3 us; the launch traced here: 88.5 us
  Pallas kernels  34.1 us (38%)
  starting transfers between devices  25.3 us (28%)
  waiting for transfers between devices  14.1 us (16%)
  local copies, waits for them, and re-layouts  11.8 us (13%)
  other arithmetic  2.36 us (3%)
    pallas_call x1, Pallas kernels, on_device(): pl.pallas_call(kept_kernel, in_specs=[IN_SMEM, IN_VMEM, IN_VMEM, IN_HBM,...  10.8 us
    all_to_all x1, starting transfers between devices, depth_gather(): lax.all_to_all(block, 'tensor', 0, 0, tiled=True, axis_index_groups=groups)  8.7 us
    unnamed x22, local copies, waits for them, and re-layouts  8.62 us
    pallas_call x1, Pallas kernels, on_device(): pl.pallas_call(momentum_pick_kernel, in_specs=[IN_SMEM] + [IN_HBM] * 3 +...  8.35 us
    all_to_all x1, waiting for transfers between devices, depth_gather(): lax.all_to_all(block, 'tensor', 0, 0, tiled=True, axis_index_groups=groups)  8 us
    all_to_all x1, starting transfers between devices, on_device(): lax.all_to_all(partial.reshape(shards, -1, 128), 'tensor', 0, 0, tiled=True)  7.65 us
    pallas_call x1, Pallas kernels, on_device(): pl.pallas_call(pick_kernel, in_specs=[IN_SMEM] + [IN_VMEM] * (RING + 2) +...  5.4 us
    pallas_call x1, Pallas kernels, on_device(): pl.pallas_call(output_kernel, in_specs=[IN_VMEM] * 3 + [IN_HBM, IN_VMEM],...  4.7 us
  transfers between devices with their start and end apart: 6, of which 4 were waited for; matrix products, arithmetic and copies ran while one was open for 6% of the time, Pallas kernels for 25%

profile of v4, /device:TPU:32, one launch (start us, length us, event | category | flops | bytes accessed | tf_op | source)
XLA Modules:
  0.0 88.5 jit_solution(13313310119517654570)
XLA Ops:
  0.6 1.7 %pack.1 = bf16[8,200,128]{2,1,0:T(8,128)(2,1)} custom-call(bf16[80,128]{1,0:T(8,128)(2,1)} %bitcast.13, bf16[80,128]{1,0:T(8,128)(2,1)} %bitcast.14, bf16[64,80]{1,0:T(8,128)(2,1)} %next_tokens.1), custom_call_target="tpu_custom_call" | custom-call | tf_op jit(solution)/shard_map/pack/pallas_call | solution.py:394
  2.3 0.0 copy-start
  2.3 0.0 copy-start.9
  2.3 8.7 %all-to-all-start = ((bf16[8,200,128]{2,1,0:T(8,128)(2,1)}), bf16[8,200,128]{2,1,0:T(8,128)(2,1)S(1)}, u32[]{:S(2)}, u32[]{:S(2)}) async-start(bf16[8,200,128]{2,1,0:T(8,128)(2,1)} %pack.1), calls=%async_computation | async-start | bytes 819200 | tf_op jit(solution)/shard_map/all_to_all | solution.py:367
  11.0 2.3 %broadcast_subtract_fusion = s32[8,7,40,32]{2,3,1,0:T(8,128)} fusion(s32[8,7,40,32]{2,3,1,0:T(8,128)} %param.18, s32[32]{0:T(128)S(1)} %iota_multiply_fusion), kind=kLoop, calls=%fused_computation | loop fusion | flops 71680 | bytes 573568 | tf_op jit(solution)/shard_map/sub | solution.py:404
  13.3 2.2 %copy.15 = s32[8,40,224]{2,1,0:T(8,128)} copy(s32[8,40,224]{1,2,0:T(8,128)} %bitcast.12) | data formatting | bytes 573440 | tf_op jit(solution)/shard_map/reshape | solution.py:405
  15.5 1.0 %pad.4.offsets.refs_9_ = s32[8,40,256]{2,1,0:T(8,128)S(1)} pad(s32[8,40,224]{2,1,0:T(8,128)} %copy.15, s32[]{:T(128)} %constant.30.clone.1), padding=0_0x0_0x0_32 | pad | bytes 614404 | tf_op jit(solution)/shard_map/jit(_pad)/pad | solution.py:406
  16.5 0.1 pad_add_fusion.place
  16.6 8.0 %all-to-all-done.piece.refs_0_ = bf16[8,200,128]{2,1,0:T(8,128)(2,1)S(1)} async-done(((bf16[8,200,128]{2,1,0:T(8,128)(2,1)}), bf16[8,200,128]{2,1,0:T(8,128)(2,1)S(1)}, u32[]{:S(2)}, u32[]{:S(2)}) %all-to-all-start) | async-done | bytes 409632 | tf_op jit(solution)/shard_map/all_to_all | solution.py:367
  24.6 2.8 %collective-permute-start.2 = (bf16[8,200,128]{2,1,0:T(8,128)(2,1)S(1)}, bf16[8,200,128]{2,1,0:T(8,128)(2,1)S(1)}, u32[]{:S(2)}, u32[]{:S(2)}) collective-permute-start(bf16[8,200,128]{2,1,0:T(8,128)(2,1)S(1)} %all-to-all-done.piece.refs_0_), channel_id=1, source_target_pairs={{0,24},{1,25},{2,26},{3,27},{4,28},{5,29},{6,30},{7,31},{8,0},{9,1... | collective-permute-start | bytes 1228808 | tf_op jit(solution)/shard_map/ppermute | solution.py:374
  27.3 0.8 collective-permute-start.1
  28.1 0.9 %collective-permute-start = (bf16[8,200,128]{2,1,0:T(8,128)(2,1)S(1)}, bf16[8,200,128]{2,1,0:T(8,128)(2,1)S(1)}, u32[]{:S(2)}, u32[]{:S(2)}) collective-permute-start(bf16[8,200,128]{2,1,0:T(8,128)(2,1)S(1)} %all-to-all-done.piece.refs_0_), channel_id=1, source_target_pairs={{0,8},{1,9},{2,10},{3,11},{4,12},{5,13},{6,14},{7,15},{8,16},{9,17... | collective-permute-start | bytes 1228808 | tf_op jit(solution)/shard_map/ppermute | solution.py:374
  29.0 0.0 copy-done
  29.0 0.0 copy-done.9
  29.0 0.0 copy-start.2
  29.0 1.2 %copy-done.2 = bf16[1024,512]{1,0:T(8,128)(2,1)S(1)} copy-done((bf16[1024,512]{1,0:T(8,128)(2,1)S(1)}, bf16[1024,512]{1,0:T(8,128)(2,1)}, u32[]{:S(2)}) %copy-start.2) | copy-done | bytes 1048600
  30.3 0.0 copy-start.6
  30.3 1.6 %copy-done.6 = bf16[2560,448]{0,1:T(8,128)(2,1)S(1)} copy-done((bf16[2560,448]{0,1:T(8,128)(2,1)S(1)}, bf16[2560,448]{0,1:T(8,128)(2,1)}, u32[]{:S(2)}) %copy-start.6) | copy-done | bytes 2293784
  31.9 0.0 copy-start.7
  31.9 1.6 %copy-done.7 = bf16[2560,448]{0,1:T(8,128)(2,1)S(1)} copy-done((bf16[2560,448]{0,1:T(8,128)(2,1)S(1)}, bf16[2560,448]{0,1:T(8,128)(2,1)}, u32[]{:S(2)}) %copy-start.7) | copy-done | bytes 2293784
  33.6 0.0 copy-start.3
  33.6 0.0 copy-start.10
  33.6 8.4 %momentum_pick.1 = (f32[40,256]{1,0:T(8,128)S(1)}, bf16[4,448,640]{2,1,0:T(8,128)(2,1)S(1)}, bf16[4,448,640]{2,1,0:T(8,128)(2,1)S(1)}, f32[448,192]{1,0:T(8,128)...) custom-call(s32[2]{0:T(128)S(1)} %pad_add_fusion.place, bf16[1,448,2560]{2,1,0:T(8,128)(2,1)S(1)} %copy-done, ...), custom_call_target="tpu_custom_call" | custom-call | flops 6000000000 | bytes 8000000 | tf_op jit(solution)/shard_map/momentum_pick/pallas_call | solution.py:413
  41.9 0.0 collective-permute-done.2.refs_3_
  41.9 0.0 collective-permute-done.1.refs_2_
  41.9 3.4 %collective-permute-done.refs_1_ = bf16[8,200,128]{2,1,0:T(8,128)(2,1)S(1)} collective-permute-done((bf16[8,200,128]{2,1,0:T(8,128)(2,1)S(1)}, bf16[8,200,128]{2,1,0:T(8,128)(2,1)S(1)}, u32[]{:S(2)}, u32[]{:S(2)}) %collective-permute-start) | collective-permute-done | bytes 409632 | tf_op jit(solution)/shard_map/ppermute | solution.py:374
  45.3 0.0 copy-done.3
  45.3 0.0 copy-done.10
  45.3 5.4 %pick.1 = (bf16[1638,80,128]{2,1,0:T(8,128)(2,1)}, bf16[448,128]{1,0:T(8,128)(2,1)S(1)}, bf16[448,64]{1,0:T(8,128)(2,1)S(1)}, bf16[8,80,128]{2,1,0:T(8,128)(2,1)}) custom-call(s32[2]{0:T(128)S(1)} %pad_add_fusion.place, bf16[8,200,128]{2,1,0:T(8,128)(2,1)S(1)} %all-to-all-done.piece.refs_0_, bf16[8,200,128]{2,1,0:T(8,128)(2,1)S(1)} %collective-permute-done.refs_1_, ...), custom_call_target="tpu_custom_call" | custom-call | flops 6000000000 | bytes 12000000 | tf_op jit(solution)/shard_map/pick/pallas_call | solution.py:433
  50.7 4.5 %all-to-all-start.1 = ((bf16[8,80,128]{2,1,0:T(8,128)(2,1)}), bf16[8,80,128]{2,1,0:T(8,128)(2,1)S(1)}, u32[]{:S(2)}, u32[]{:S(2)}) async-start(bf16[8,80,128]{2,1,0:T(8,128)(2,1)} %get-tuple-element.20.sent), calls=%async_computation.1 | async-start | bytes 327680 | tf_op jit(solution)/shard_map/all_to_all | solution.py:460
  55.2 0.0 copy-start.4
  55.2 1.2 %copy-done.4 = bf16[1024,512]{1,0:T(8,128)(2,1)S(1)} copy-done((bf16[1024,512]{1,0:T(8,128)(2,1)S(1)}, bf16[1024,512]{1,0:T(8,128)(2,1)}, u32[]{:S(2)}) %copy-start.4) | copy-done | bytes 1048600
  56.4 0.0 copy-start.8
  56.4 1.6 %copy-done.8 = bf16[448,2560]{1,0:T(8,128)(2,1)S(1)} copy-done((bf16[448,2560]{1,0:T(8,128)(2,1)S(1)}, bf16[448,2560]{1,0:T(8,128)(2,1)}, u32[]{:S(2)}) %copy-start.8) | copy-done | bytes 2293784
  58.1 0.0 copy-start.1
  58.1 2.6 %next_rows.1 = (f32[3276,2560]{1,0:T(8,128)}, bf16[512,128]{1,0:T(8,128)(2,1)S(1)}) custom-call(bf16[448,64]{1,0:T(8,128)(2,1)S(1)} %get-tuple-element.21.next_hidden, bf16[448,2560]{1,0:T(8,128)(2,1)S(1)} %copy-done.8, bf16[1024,512]{1,0:T(8,128)(2,1)S(1)} %copy-done.4), custom_call_target="tpu_custom_call" | custom-call | flops 2000000000 | bytes 7000000 | tf_op jit(solution)/shard_map/next_rows/pallas_call | solution.py:462
  60.7 1.0 %all-to-all-done.1.values = bf16[8,80,128]{2,1,0:T(8,128)(2,1)S(1)} async-done(((bf16[8,80,128]{2,1,0:T(8,128)(2,1)}), bf16[8,80,128]{2,1,0:T(8,128)(2,1)S(1)}, u32[]{:S(2)}, u32[]{:S(2)}) %all-to-all-start.1) | async-done | bytes 163872 | tf_op jit(solution)/shard_map/all_to_all | solution.py:460
  61.7 0.0 copy-done.1
  61.7 4.7 %output_part.1 = bf16[1280,128]{1,0:T(8,128)(2,1)} custom-call(bf16[8,80,128]{2,1,0:T(8,128)(2,1)S(1)} %all-to-all-done.1.values, s32[8,40,256]{2,1,0:T(8,128)S(1)} %pad.4.offsets.refs_9_, bf16[512,128]{1,0:T(8,128)(2,1)S(1)} %get-tuple-element.22.next_rows, f32[3276,2560]{1,0:T(8,128)} %get-tuple-element.23.base_whole, bf16[256,512]{1,0:T(8,128)(2,1)S(1)} %copy-done.1), custom_call_target="tpu_custom_call" | custom-call | flops 4000000000 | bytes 4000000 | tf_op jit(solution)/shard_map/output_part/pallas_call | solution.py:478
  66.4 7.7 %all-to-all-start.2 = ((bf16[32,40,128]{2,1,0:T(8,128)(2,1)}), bf16[32,40,128]{2,1,0:T(8,128)(2,1)S(1)}, u32[]{:S(2)}, u32[]{:S(2)}) async-start(bf16[32,40,128]{2,1,0:T(8,128)(2,1)} %bitcast.8), calls=%async_computation.2 | async-start | bytes 655360 | tf_op jit(solution)/shard_map/all_to_all | solution.py:496
  74.1 0.0 copy-start.5
  74.1 1.2 %copy-done.5 = bf16[1024,512]{1,0:T(8,128)(2,1)S(1)} copy-done((bf16[1024,512]{1,0:T(8,128)(2,1)S(1)}, bf16[1024,512]{1,0:T(8,128)(2,1)}, u32[]{:S(2)}) %copy-start.5) | copy-done | bytes 1048600
  75.3 10.8 %kept.1 = bf16[1,448,2560]{2,1,0:T(8,128)(2,1)} custom-call(s32[2]{0:T(128)S(1)} %pad_add_fusion.place, bf16[8,80,128]{2,1,0:T(8,128)(2,1)} %get-tuple-element.20.sent, s32[8,40,256]{2,1,0:T(8,128)S(1)} %pad.4.offsets.refs_9_, bf16[1638,80,128]{2,1,0:T(8,128)(2,1)} %get-tuple-element.24.whole_grads, bf16[448,128]{1,0:T(8,128)(2,1)S(1)} %get-tuple-element.25.hidden, ...), custom_call_target="tpu_custom_call" | custom-call | flops 10000000000 | bytes 8000000 | tf_op jit(solution)/shard_map/kept/pallas_call | solution.py:506
  86.1 1.7 %all-to-all-done.2.received = bf16[32,40,128]{2,1,0:T(8,128)(2,1)S(1)} async-done(((bf16[32,40,128]{2,1,0:T(8,128)(2,1)}), bf16[32,40,128]{2,1,0:T(8,128)(2,1)S(1)}, u32[]{:S(2)}, u32[]{:S(2)}) %all-to-all-start.2) | async-done | bytes 327712 | tf_op jit(solution)/shard_map/all_to_all | solution.py:496
  87.8 0.7 output_sum.1
  (1 shorter events, 0.0 us)
Async XLA Ops:
  2.3 26.7 %copy-start = (bf16[1,448,2560]{2,1,0:T(8,128)(2,1)S(1)}, bf16[1,448,2560]{2,1,0:T(8,128)(2,1)}, u32[]{:S(2)}) copy-start(bf16[1,448,2560]{2,1,0:T(8,128)(2,1)} %momentum.3) | copy-start | bytes 6881284
  2.3 26.7 %copy-start.9 = (bf16[256,512]{1,0:T(8,128)(2,1)S(1)}, bf16[256,512]{1,0:T(8,128)(2,1)}, u32[]{:S(2)}) copy-start(bf16[256,512]{1,0:T(8,128)(2,1)} %constant.35.clone.band.refs_7_) | copy-start | bytes 786436
  2.3 22.3 %all-to-all-start = ((bf16[8,200,128]{2,1,0:T(8,128)(2,1)}), bf16[8,200,128]{2,1,0:T(8,128)(2,1)S(1)}, u32[]{:S(2)}, u32[]{:S(2)}) async-start(bf16[8,200,128]{2,1,0:T(8,128)(2,1)} %pack.1), calls=%async_computation | async-start | bytes 819200 | tf_op jit(solution)/shard_map/all_to_all | solution.py:367
  24.6 17.3 %collective-permute-start.2 = (bf16[8,200,128]{2,1,0:T(8,128)(2,1)S(1)}, bf16[8,200,128]{2,1,0:T(8,128)(2,1)S(1)}, u32[]{:S(2)}, u32[]{:S(2)}) collective-permute-start(bf16[8,200,128]{2,1,0:T(8,128)(2,1)S(1)} %all-to-all-done.piece.refs_0_), channel_id=1, source_target_pairs={{0,24},{1,25},{2,26},{3,27},{4,28},{5,29},{6,30},{7,31},{8,0},{9,1... | collective-permute-start | bytes 1228808 | tf_op jit(solution)/shard_map/ppermute | solution.py:374
  27.3 14.6 %collective-permute-start.1 = (bf16[8,200,128]{2,1,0:T(8,128)(2,1)S(1)}, bf16[8,200,128]{2,1,0:T(8,128)(2,1)S(1)}, u32[]{:S(2)}, u32[]{:S(2)}) collective-permute-start(bf16[8,200,128]{2,1,0:T(8,128)(2,1)S(1)} %all-to-all-done.piece.refs_0_), channel_id=1, source_target_pairs={{0,16},{1,17},{2,18},{3,19},{4,20},{5,21},{6,22},{7,23},{8,24},{9,... | collective-permute-start | bytes 1228808 | tf_op jit(solution)/shard_map/ppermute | solution.py:374
  28.1 17.2 %collective-permute-start = (bf16[8,200,128]{2,1,0:T(8,128)(2,1)S(1)}, bf16[8,200,128]{2,1,0:T(8,128)(2,1)S(1)}, u32[]{:S(2)}, u32[]{:S(2)}) collective-permute-start(bf16[8,200,128]{2,1,0:T(8,128)(2,1)S(1)} %all-to-all-done.piece.refs_0_), channel_id=1, source_target_pairs={{0,8},{1,9},{2,10},{3,11},{4,12},{5,13},{6,14},{7,15},{8,16},{9,17... | collective-permute-start | bytes 1228808 | tf_op jit(solution)/shard_map/ppermute | solution.py:374
  29.0 1.2 %copy-start.2 = (bf16[1024,512]{1,0:T(8,128)(2,1)S(1)}, bf16[1024,512]{1,0:T(8,128)(2,1)}, u32[]{:S(2)}) copy-start(bf16[1024,512]{1,0:T(8,128)(2,1)} %constant.34.clone.row_pair.refs_6_) | copy-start | bytes 3145732
  30.3 1.6 %copy-start.6 = (bf16[2560,448]{0,1:T(8,128)(2,1)S(1)}, bf16[2560,448]{0,1:T(8,128)(2,1)}, u32[]{:S(2)}) copy-start(bf16[2560,448]{0,1:T(8,128)(2,1)} %param.14) | copy-start | bytes 6881284
  31.9 1.6 %copy-start.7 = (bf16[2560,448]{0,1:T(8,128)(2,1)S(1)}, bf16[2560,448]{0,1:T(8,128)(2,1)}, u32[]{:S(2)}) copy-start(bf16[2560,448]{0,1:T(8,128)(2,1)} %param.15) | copy-start | bytes 6881284
  33.6 11.7 %copy-start.3 = (bf16[1024,512]{1,0:T(8,128)(2,1)S(1)}, bf16[1024,512]{1,0:T(8,128)(2,1)}, u32[]{:S(2)}) copy-start(bf16[1024,512]{1,0:T(8,128)(2,1)} %constant.34.clone.row_pair.refs_6_) | copy-start | bytes 3145732
  33.6 11.7 %copy-start.10 = (bf16[256,512]{1,0:T(8,128)(2,1)S(1)}, bf16[256,512]{1,0:T(8,128)(2,1)}, u32[]{:S(2)}) copy-start(bf16[256,512]{1,0:T(8,128)(2,1)} %constant.35.clone.band.refs_7_) | copy-start | bytes 786436
  50.7 11.0 %all-to-all-start.1 = ((bf16[8,80,128]{2,1,0:T(8,128)(2,1)}), bf16[8,80,128]{2,1,0:T(8,128)(2,1)S(1)}, u32[]{:S(2)}, u32[]{:S(2)}) async-start(bf16[8,80,128]{2,1,0:T(8,128)(2,1)} %get-tuple-element.20.sent), calls=%async_computation.1 | async-start | bytes 327680 | tf_op jit(solution)/shard_map/all_to_all | solution.py:460
  55.2 1.2 %copy-start.4 = (bf16[1024,512]{1,0:T(8,128)(2,1)S(1)}, bf16[1024,512]{1,0:T(8,128)(2,1)}, u32[]{:S(2)}) copy-start(bf16[1024,512]{1,0:T(8,128)(2,1)} %constant.34.clone.row_pair.refs_6_) | copy-start | bytes 3145732
  56.4 1.6 %copy-start.8 = (bf16[448,2560]{1,0:T(8,128)(2,1)S(1)}, bf16[448,2560]{1,0:T(8,128)(2,1)}, u32[]{:S(2)}) copy-start(bf16[448,2560]{1,0:T(8,128)(2,1)} %down.1) | copy-start | bytes 6881284
  58.1 3.6 %copy-start.1 = (bf16[256,512]{1,0:T(8,128)(2,1)S(1)}, bf16[256,512]{1,0:T(8,128)(2,1)}, u32[]{:S(2)}) copy-start(bf16[256,512]{1,0:T(8,128)(2,1)} %constant.36.clone.back) | copy-start | bytes 786436
  66.4 21.4 %all-to-all-start.2 = ((bf16[32,40,128]{2,1,0:T(8,128)(2,1)}), bf16[32,40,128]{2,1,0:T(8,128)(2,1)S(1)}, u32[]{:S(2)}, u32[]{:S(2)}) async-start(bf16[32,40,128]{2,1,0:T(8,128)(2,1)} %bitcast.8), calls=%async_computation.2 | async-start | bytes 655360 | tf_op jit(solution)/shard_map/all_to_all | solution.py:496
  74.1 1.2 %copy-start.5 = (bf16[1024,512]{1,0:T(8,128)(2,1)S(1)}, bf16[1024,512]{1,0:T(8,128)(2,1)}, u32[]{:S(2)}) copy-start(bf16[1024,512]{1,0:T(8,128)(2,1)} %constant.34.clone.row_pair.refs_6_) | copy-start | bytes 3145732
